TPU v7x, 32 devices: a whole 2x2x4 slice. The times are simulated.
32 devices in a mesh: query: 4 (over y, x), cluster: 8 (over z, core).
Axes of the slice: x: 2, y: 2, z: 4, core: 2. Of those that a mesh axis runs over, the one named last changes fastest.
Arguments:
- queries: bfloat16 [1024, 512], P(('query', 'cluster')), may hold values from -68 to 68
- centroids: bfloat16 [64, 512], P('cluster'), may hold values from -6 to 6
- leaves: bfloat16 [64, 1024, 512], P('cluster'), may hold values from -5 to 5
- beam: int32 [1024, 8], P('query'), may hold values from 0 to 63, all different within a row; in each aligned block of 256 rows (0 to 255, 256 to 511, ...) at most 64 rows name the same one
Outputs:
- readout: bfloat16 [1024, 512], P(('query', 'cluster'))
- beam_logprob: float32 [1024, 8], P(('query', 'cluster'))
Inputs may be any that keep to these rules, and one draw needn't show every extreme that they name: `beam`: each row names 8 different clusters. In each aligned block of 256 rows (the queries of one index of query) no cluster is named by more than 64 rows, a bound that some block reaches.
All inputs are finite; a program needn't handle non-finite values.
Results may differ from a plain program's by a relative error of at most 0.0028.
Values may be sent and summed in bfloat16 or wider, within the bound.
A program may use at most 128 MiB of HBM per device.

v0:
```python
import math

import jax
import jax.numpy as jnp
from jax import lax
from jax.sharding import PartitionSpec as P

floor_value = -1e30


def merged_2(part, axis, combine):
    gathered = jax.tree.map(lambda a: lax.all_gather(a, axis), part)

    def take(source):
        return jax.tree.map(lambda a: lax.dynamic_index_in_dim(a, source, 0, False), gathered)

    return lax.fori_loop(
        1, lax.axis_size(axis), lambda source, state: combine(state, take(source)), take(0)
    )


def combine_states(first, second):
    cmax_one, csum_one, beam_one, lmax_one, lsum_one, accum_one = first
    cmax_two, csum_two, beam_two, lmax_two, lsum_two, accum_two = second
    cmax_new = jnp.maximum(cmax_one, cmax_two)
    csum_new = csum_one * jnp.exp(cmax_one - cmax_new) + csum_two * jnp.exp(cmax_two - cmax_new)
    lmax_new = jnp.maximum(lmax_one, lmax_two)
    factor_one = jnp.exp(lmax_one - lmax_new)
    factor_two = jnp.exp(lmax_two - lmax_new)
    lsum_new = lsum_one * factor_one + lsum_two * factor_two
    accum_new = accum_one * factor_one[:, None] + accum_two * factor_two[:, None]
    return (cmax_new, csum_new, beam_one + beam_two, lmax_new, lsum_new, accum_new)


def per_device(queries, centroids, leaves, beam):
    groups = lax.axis_size("cluster")
    query_block = lax.all_gather(queries, "cluster", axis=0, tiled=True)
    query_count, model_width = query_block.shape
    cluster_count, leaf_count, unused_width = leaves.shape
    beam_width = beam.shape[1]
    score_scale = 1.0 / math.sqrt(model_width)
    first_cluster = lax.axis_index("cluster") * cluster_count
    cscore = jnp.dot(query_block, centroids.T, preferred_element_type=jnp.float32) * score_scale
    cmax_part = jnp.max(cscore, axis=1)
    csum_part = jnp.sum(jnp.exp(cscore - cmax_part[:, None]), axis=1)
    owned = first_cluster + jnp.arange(cluster_count, dtype=jnp.int32)
    matches = beam[:, :, None] == owned[None, None, :]
    beam_part = jnp.sum(jnp.where(matches, cscore[:, None, :], 0.0), axis=2)
    membership = jnp.any(matches, axis=1).astype(jnp.int32)
    slot_index = jnp.cumsum(membership, axis=0) - 1
    capacity = max(4, 2 * query_count * beam_width // (cluster_count * groups))
    positions = jnp.arange(capacity, dtype=jnp.int32)
    dispatch = (membership.T[:, None, :] == 1) & (
        slot_index.T[:, None, :] == positions[None, :, None]
    )
    picked = jnp.einsum(
        "csq,qd->csd",
        dispatch.astype(jnp.bfloat16),
        query_block,
        preferred_element_type=jnp.float32,
    ).astype(jnp.bfloat16)
    slot_centroid = jnp.sum(jnp.where(dispatch, cscore.T[:, None, :], 0.0), axis=2)
    logits = (
        jnp.einsum("csd,cjd->csj", picked, leaves, preferred_element_type=jnp.float32) * score_scale
    )
    logits = logits + slot_centroid[:, :, None]
    slot_max = jnp.max(logits, axis=2)
    weights = jnp.exp(logits - slot_max[:, :, None])
    slot_sum = jnp.sum(weights, axis=2)
    slot_accum = jnp.einsum(
        "csj,cjd->csd", weights.astype(jnp.bfloat16), leaves, preferred_element_type=jnp.float32
    )
    slot_total = cluster_count * capacity
    dispatch_flat = dispatch.reshape(slot_total, query_count)
    slot_max_flat = slot_max.reshape(slot_total)
    masked_max = jnp.where(dispatch_flat, slot_max_flat[:, None], floor_value)
    lmax_part = jnp.max(masked_max, axis=0)
    exponent = jnp.where(dispatch_flat, slot_max_flat[:, None] - lmax_part[None, :], 0.0)
    factors = jnp.where(dispatch_flat, jnp.exp(exponent), 0.0)
    lsum_part = jnp.sum(factors * slot_sum.reshape(slot_total)[:, None], axis=0)
    accum_part = jnp.dot(
        factors.T,
        slot_accum.reshape(slot_total, model_width),
        precision=lax.Precision.HIGHEST,
        preferred_element_type=jnp.float32,
    )
    state = (cmax_part, csum_part, beam_part, lmax_part, lsum_part, accum_part)
    row_count = query_count // groups
    merged = merged_2(state, "cluster", combine_states)
    row_start = lax.axis_index("cluster") * row_count
    own = tuple((lax.dynamic_slice_in_dim(member, row_start, row_count, 0) for member in merged))
    cmax_own, csum_own, beam_own, lmax_own, lsum_own, accum_own = own
    lse = cmax_own + jnp.log(csum_own)
    beam_logprob = beam_own - lse[:, None]
    readout = (accum_own / lsum_own[:, None]).astype(jnp.bfloat16)
    return (readout, beam_logprob)


def solution(mesh):
    return jax.shard_map(
        per_device,
        mesh=mesh,
        in_specs=(
            P(("query", "cluster"), None),
            P("cluster", None),
            P("cluster", None, None),
            P("query", None),
        ),
        out_specs=(P(("query", "cluster"), None), P(("query", "cluster"), None)),
        check_vma=False,
    )
```

profile of v0, /device:TPU:0, one launch (start us, length us, event | category | flops | bytes accessed | tf_op | source)
XLA Modules:
  0.0 112.4 jit_solution(3446280840085519060)
XLA Ops:
  7.2 0.8 compare_reduce_fusion
  8.0 0.6 reduce-window.6
  9.0 16.1 %all_gather.39 = bf16[256,512]{1,0:T(8,128)(2,1)S(1)} all-gather(bf16[32,512]{1,0:T(8,128)(2,1)} %param.6), channel_id=1, replica_groups=mesh['query'=4,'cluster'=8] {'cluster'}, dimensions={0}, use_global_device_ids=true | all-gather | bytes 294912 | tf_op jit(solution)/shard_map/all_gather | solution.py:37
  25.4 5.3 %fusion.1 = (f32[8,64]{1,0:T(8,128)S(1)}, f32[8,64,1024]{2,1,0:T(8,128)S(1)}) fusion(f32[8,64]{1,0:T(8,128)S(1)} %select_reduce_fusion.1, bf16[8,1024,512]{2,1,0:T(8,128)(2,1)} %param.8, bf16[256,512]{1,0:T(8,128)(2,1)S(1)} %all_gather.39, s32[8,256]{1,0:T(8,128)S(1)} %add_bitcast_fusion, pred[8,256]{1,0:T(8,128)(4,1)S(1)} %fusion.26), kind=kOutput, calls=%fused_computation.13 | convolution fusion | flops 673185280 | bytes 10762240 | tf_op jit(solution)/shard_map/csd,cjd->csj/dot_general | solution.py:64
  31.0 4.9 %fusion.5 = f32[8,64,512]{2,1,0:T(8,128)S(1)} fusion(bf16[8,1024,512]{2,1,0:T(8,128)(2,1)} %param.8, f32[8,64,1024]{2,1,0:T(8,128)S(1)} %get-tuple-element.358, f32[8,64]{1,0:T(8,128)S(1)} %get-tuple-element.357, f32[8,64]{1,0:T(8,128)S(1)} %select_reduce_fusion.1), kind=kOutput, calls=%fused_computation.20 | convolution fusion | flops 538968064 | bytes 11538432 | tf_op jit(solution)/shard_map/csj,cjd->csd/dot_general | solution.py:70
  35.9 2.1 %convolution_bitcast_fusion = f32[256,512]{1,0:T(8,128)} fusion(f32[8,64,512]{2,1,0:T(8,128)S(1)} %fusion.5, f32[256]{0:T(256)S(1)} %select_reduce_fusion, f32[8,64]{1,0:T(8,128)S(1)} %get-tuple-element.357, s32[8,256]{1,0:T(8,128)S(1)} %add_bitcast_fusion, pred[8,256]{1,0:T(8,128)(4,1)S(1)} %fusion.26), kind=kOutput, calls=%fused_computation.18 | convolution fusion | flops 805961728 | bytes 1586176 | tf_op jit(solution)/shard_map/dot_general | solution.py:81
  38.0 11.8 %all-gather.7 = f32[8,1,256]{2,1,0:T(1,128)S(1)} all-gather(f32[1,1,256]{2,1,0:T(1,128)S(1)} %bitcast.83), channel_id=3, replica_groups=mesh['query'=4,'cluster'=8] {'cluster'}, dimensions={0}, use_global_device_ids=true | all-gather | bytes 9216 | tf_op jit(solution)/shard_map/all_gather | solution.py:12
  49.8 8.9 %all-gather.6 = f32[8,1,256]{2,1,0:T(1,128)S(1)} all-gather(f32[1,1,256]{2,1,0:T(1,128)S(1)} %bitcast.82), channel_id=2, replica_groups=mesh['query'=4,'cluster'=8] {'cluster'}, dimensions={0}, use_global_device_ids=true | all-gather | bytes 9216 | tf_op jit(solution)/shard_map/all_gather | solution.py:12
  58.7 0.6 fusion.3
  59.3 0.3 multiply_reduce_fusion
  59.6 10.9 %all-gather.9 = f32[8,1,256]{2,1,0:T(1,128)S(1)} all-gather(f32[1,1,256]{2,1,0:T(1,128)S(1)} %bitcast.85), channel_id=6, replica_groups=mesh['query'=4,'cluster'=8] {'cluster'}, dimensions={0}, use_global_device_ids=true | all-gather | bytes 9216 | tf_op jit(solution)/shard_map/all_gather | solution.py:12
  70.5 8.9 %all-gather.8 = f32[8,1,256]{2,1,0:T(1,128)S(1)} all-gather(f32[1,1,256]{2,1,0:T(1,128)S(1)} %bitcast.84), channel_id=5, replica_groups=mesh['query'=4,'cluster'=8] {'cluster'}, dimensions={0}, use_global_device_ids=true | all-gather | bytes 9216 | tf_op jit(solution)/shard_map/all_gather | solution.py:12
  79.5 13.9 %all-gather.2 = f32[2048,8]{0,1:T(8,128)S(1)} all-gather(f32[256,8]{0,1:T(8,128)S(1)} %fusion.25), channel_id=4, replica_groups=mesh['query'=4,'cluster'=8] {'cluster'}, dimensions={0}, use_global_device_ids=true | all-gather | bytes 73728 | tf_op jit(solution)/shard_map/all_gather | solution.py:12
  93.5 1.1 slice.30
  94.5 9.4 %while.25 = (s32[]{:T(128)}, f32[256]{0:T(256)S(1)}, f32[256]{0:T(256)S(1)}, f32[256,8]{0,1:T(8,128)S(1)}, f32[256]{0:T(256)S(1)}, /*index=5*/f32[256]{0:T(256)S...) while((s32[]{:T(128)}, f32[256]{0:T(256)S(1)}, ...), condition=%wide.region_12.13_spmd, body=%wide.region_11.12_spmd.sunk | while | flops 398341 | bytes 1622215 | solution.py:17
  94.6 1.2 %fusion.40 = f32[256,512]{1,0:T(8,128)S(1)} fusion(f32[8,256,512]{2,1,0:T(8,128)} %get-tuple-element.502, s32[]{:T(128)S(6)} %select_n.75, f32[256,512]{1,0:T(8,128)S(1)} %get-tuple-element.480, f32[256]{0:T(256)S(1)} %get-tuple-element.456, f32[256]{0:T(256)S(1)} %get-tuple-element.457), kind=kLoop, calls=%fused_computation.1.clone.1 | loop fusion | flops 393216 | bytes 1574916 | tf_op jit(solution)/shard_map/while/body/eval_jaxpr/add | solution.py:31
  96.0 1.2 %fusion.40 = f32[256,512]{1,0:T(8,128)S(1)} fusion(f32[8,256,512]{2,1,0:T(8,128)} %get-tuple-element.502, s32[]{:T(128)S(6)} %select_n.75, f32[256,512]{1,0:T(8,128)S(1)} %get-tuple-element.480, f32[256]{0:T(256)S(1)} %get-tuple-element.456, f32[256]{0:T(256)S(1)} %get-tuple-element.457), kind=kLoop, calls=%fused_computation.1.clone.1 | loop fusion | flops 393216 | bytes 1574916 | tf_op jit(solution)/shard_map/while/body/eval_jaxpr/add | solution.py:31
  97.3 1.2 %fusion.40 = f32[256,512]{1,0:T(8,128)S(1)} fusion(f32[8,256,512]{2,1,0:T(8,128)} %get-tuple-element.502, s32[]{:T(128)S(6)} %select_n.75, f32[256,512]{1,0:T(8,128)S(1)} %get-tuple-element.480, f32[256]{0:T(256)S(1)} %get-tuple-element.456, f32[256]{0:T(256)S(1)} %get-tuple-element.457), kind=kLoop, calls=%fused_computation.1.clone.1 | loop fusion | flops 393216 | bytes 1574916 | tf_op jit(solution)/shard_map/while/body/eval_jaxpr/add | solution.py:31
  98.7 1.2 %fusion.40 = f32[256,512]{1,0:T(8,128)S(1)} fusion(f32[8,256,512]{2,1,0:T(8,128)} %get-tuple-element.502, s32[]{:T(128)S(6)} %select_n.75, f32[256,512]{1,0:T(8,128)S(1)} %get-tuple-element.480, f32[256]{0:T(256)S(1)} %get-tuple-element.456, f32[256]{0:T(256)S(1)} %get-tuple-element.457), kind=kLoop, calls=%fused_computation.1.clone.1 | loop fusion | flops 393216 | bytes 1574916 | tf_op jit(solution)/shard_map/while/body/eval_jaxpr/add | solution.py:31
  100.0 1.2 %fusion.40 = f32[256,512]{1,0:T(8,128)S(1)} fusion(f32[8,256,512]{2,1,0:T(8,128)} %get-tuple-element.502, s32[]{:T(128)S(6)} %select_n.75, f32[256,512]{1,0:T(8,128)S(1)} %get-tuple-element.480, f32[256]{0:T(256)S(1)} %get-tuple-element.456, f32[256]{0:T(256)S(1)} %get-tuple-element.457), kind=kLoop, calls=%fused_computation.1.clone.1 | loop fusion | flops 393216 | bytes 1574916 | tf_op jit(solution)/shard_map/while/body/eval_jaxpr/add | solution.py:31
  101.4 1.2 %fusion.40 = f32[256,512]{1,0:T(8,128)S(1)} fusion(f32[8,256,512]{2,1,0:T(8,128)} %get-tuple-element.502, s32[]{:T(128)S(6)} %select_n.75, f32[256,512]{1,0:T(8,128)S(1)} %get-tuple-element.480, f32[256]{0:T(256)S(1)} %get-tuple-element.456, f32[256]{0:T(256)S(1)} %get-tuple-element.457), kind=kLoop, calls=%fused_computation.1.clone.1 | loop fusion | flops 393216 | bytes 1574916 | tf_op jit(solution)/shard_map/while/body/eval_jaxpr/add | solution.py:31
  102.7 1.2 %fusion.40 = f32[256,512]{1,0:T(8,128)S(1)} fusion(f32[8,256,512]{2,1,0:T(8,128)} %get-tuple-element.502, s32[]{:T(128)S(6)} %select_n.75, f32[256,512]{1,0:T(8,128)S(1)} %get-tuple-element.480, f32[256]{0:T(256)S(1)} %get-tuple-element.456, f32[256]{0:T(256)S(1)} %get-tuple-element.457), kind=kLoop, calls=%fused_computation.1.clone.1 | loop fusion | flops 393216 | bytes 1574916 | tf_op jit(solution)/shard_map/while/body/eval_jaxpr/add | solution.py:31
  104.1 0.7 divide_convert_fusion
  104.8 0.7 dynamic-slice_subtract_fusion
  (65 shorter events, 1.7 us)
Async XLA Ops:
  7.2 17.9 %copy-start = (bf16[8,512]{1,0:T(8,128)(2,1)S(1)}, bf16[8,512]{1,0:T(8,128)(2,1)}, u32[]{:S(2)}) copy-start(bf16[8,512]{1,0:T(8,128)(2,1)} %param.7) | copy-start | bytes 24580
  7.2 86.3 %all-gather.12.cloned.1.call-start = ((), (), s32[]{:S(2)}) async-start(), calls=%async_computation | async-start | bytes 4718592 | tf_op jit(solution)/shard_map/all_gather | solution.py:12
  35.8 43.6 %copy-start.1 = (s32[256,8]{0,1:T(8,128)S(1)}, s32[256,8]{0,1:T(8,128)}, u32[]{:S(2)}) copy-start(s32[256,8]{0,1:T(8,128)} %param.9) | copy-start | bytes 24580
Sparse Core Ops, SparseCore 0:
  38.1 48.4 all-gather.11
where the time goes:
time: 113 us; the launch traced here: 112 us
  blocking collectives  70.6 us (62%)
  between operations  14.1 us (12%)
  other arithmetic  13.2 us (12%)
  matrix products  12.5 us (11%)
  local copies, waits for them, and re-layouts  1.53 us (1%)
    all_gather x5, blocking collectives, merged_2(): gathered = jax.tree.map(lambda a: lax.all_gather(a, axis), part)  54.5 us
    all_gather x1, blocking collectives, per_device(): query_block = lax.all_gather(queries, 'cluster', axis=0, tiled=True)  16.1 us
    add x7, other arithmetic, combine_states(): accum_one * factor_one[:, None] + accum_two * factor_two[:, None]  8.6 us
    dot_general x1, matrix products, per_device(): jnp.einsum('csd,cjd->csj', picked, leaves, preferred_element_type=jnp.flo...  5.34 us
    dot_general x1, matrix products, per_device(): jnp.einsum('csj,cjd->csd', weights.astype(jnp.bfloat16), leaves, preferre...  4.89 us
  transfers between devices with their start and end apart: 1, of which 0 were waited for; matrix products, arithmetic and copies ran while one was open for 1% of the time, Pallas kernels for 0%

commit v1 on v0

--- a/solution.py
+++ b/solution.py
@@ -1,8 +1,11 @@
+import functools
 import math
 
 import jax
 import jax.numpy as jnp
 from jax import lax
+from jax.experimental import pallas as pl
+from jax.experimental.pallas import tpu as pltpu
 from jax.sharding import PartitionSpec as P
 
 floor_value = -1e30
@@ -96,9 +99,303 @@
     return (readout, beam_logprob)
 
 
+MESH = pl.DeviceIdType.MESH
+CODE_MAX = 32767.0
+LANES = 128
+
+
+def fused_kernel(
+    groups,
+    q_ref,
+    cent_ref,
+    leaves_ref,
+    beam_ref,
+    readout_ref,
+    logprob_ref,
+    block,
+    leaf_buf,
+    cscore_send,
+    cscore_recv,
+    stat_send,
+    stat_recv,
+    code_send,
+    code_recv,
+    accum,
+    leaf_sem,
+    own_sem,
+    q_send_sem,
+    q_recv_sem,
+    cscore_send_sem,
+    cscore_recv_sem,
+    stat_send_sem,
+    stat_recv_sem,
+    code_send_sem,
+    code_recv_sem,
+):
+    rows, width = q_ref.shape
+    clusters = cent_ref.shape[0]
+    total = groups * rows
+    beam_width = beam_ref.shape[1]
+    chips = groups // 2
+    score_scale = 1.0 / math.sqrt(width)
+    me = lax.axis_index("cluster")
+    chip, core = me // 2, me % 2
+    sibling = chip * 2 + (1 - core)
+    first = me * clusters
+
+    def peer_at(offset, side):
+        return lax.rem(chip + offset, chips) * 2 + side
+
+    peers = [peer_at(o, s) for o in range(1, chips) for s in (core, 1 - core)] + [sibling]
+
+    leaf_copies = [
+        pltpu.make_async_copy(leaves_ref.at[c], leaf_buf.at[c], leaf_sem.at[c])
+        for c in range(clusters)
+    ]
+    for copy in leaf_copies:
+        copy.start()
+    own_copy = pltpu.make_async_copy(q_ref, block.at[me], own_sem)
+    own_copy.start()
+
+    barrier = pltpu.get_barrier_semaphore()
+    for peer in peers:
+        pl.semaphore_signal(barrier, inc=1, device_id={"cluster": peer}, device_id_type=MESH)
+    pl.semaphore_wait(barrier, len(peers))
+
+    def push(src, dst, send_sem, recv_sem, peer):
+        return pltpu.make_async_remote_copy(
+            src_ref=src,
+            dst_ref=dst,
+            send_sem=send_sem,
+            recv_sem=recv_sem,
+            device_id={"cluster": peer},
+            device_id_type=MESH,
+        )
+
+    sends = []
+    for number, offset in enumerate(range(1, chips)):
+        peer = peer_at(offset, core)
+        sends.append(push(q_ref, block.at[me], q_send_sem.at[number], q_recv_sem.at[me], peer))
+    sends.append(push(q_ref, block.at[me], q_send_sem.at[chips - 1], q_recv_sem.at[me], sibling))
+    for copy in sends:
+        copy.start()
+
+    def arrival(origin):
+        return push(block.at[origin], block.at[origin], q_send_sem.at[0], q_recv_sem.at[origin], sibling)
+
+    for offset in range(1, chips):
+        origin = peer_at(chips - offset, core)
+        arrival(origin).wait_recv()
+        relay = push(
+            block.at[origin],
+            block.at[origin],
+            q_send_sem.at[chips - 1 + offset],
+            q_recv_sem.at[origin],
+            sibling,
+        )
+        relay.start()
+        sends.append(relay)
+    arrival(sibling).wait_recv()
+    for offset in range(1, chips):
+        arrival(peer_at(chips - offset, 1 - core)).wait_recv()
+    own_copy.wait()
+
+    queries = block[...].reshape(total, width)
+    lane = lax.broadcasted_iota(jnp.int32, (total, LANES), 1)
+    cent = jnp.concatenate(
+        [cent_ref[...], jnp.zeros((LANES - clusters, width), cent_ref.dtype)], axis=0
+    )
+    nt = (((1,), (1,)), ((), ()))
+    cscore = lax.dot_general(queries, cent, nt, preferred_element_type=jnp.float32) * score_scale
+    cscore_send[...] = cscore.reshape(groups, rows, LANES)
+
+    cscore_copies = []
+    for number, peer in enumerate(peers):
+        cscore_copies.append(
+            push(
+                cscore_send.at[peer],
+                cscore_recv.at[me],
+                cscore_send_sem.at[number],
+                cscore_recv_sem.at[me],
+                peer,
+            )
+        )
+    for copy in cscore_copies:
+        copy.start()
+
+    beams = beam_ref[...]
+    top = jnp.full((total, 1), floor_value, jnp.float32)
+    denom = jnp.zeros((total, 1), jnp.float32)
+
+    def scores(c):
+        leaf_copies[c].wait()
+        return lax.dot_general(queries, leaf_buf[c], nt, preferred_element_type=jnp.float32)
+
+    current = scores(0)
+    for c in range(clusters):
+        upcoming = scores(c + 1) if c + 1 < clusters else None
+        member = jnp.max((beams == first + c).astype(jnp.float32), axis=1, keepdims=True) > 0.0
+        centroid = jnp.sum(jnp.where(lane == c, cscore, 0.0), axis=1, keepdims=True)
+        peak = jnp.max(current, axis=1, keepdims=True)
+        weights = jnp.exp((current - peak) * score_scale)
+        mass = jnp.sum(weights, axis=1, keepdims=True)
+        summed = jnp.dot(
+            weights.astype(jnp.bfloat16), leaf_buf[c], preferred_element_type=jnp.float32
+        )
+        level = jnp.where(member, peak * score_scale + centroid, floor_value)
+        raised = jnp.maximum(top, level)
+        keep = jnp.exp(top - raised)
+        gain = jnp.where(member, jnp.exp(level - raised), 0.0)
+        denom = denom * keep + mass * gain
+        if c == 0:
+            accum[...] = summed * gain
+        else:
+            accum[...] = accum[...] * keep + summed * gain
+        top = raised
+        current = upcoming
+
+    held = accum[...]
+    largest = jnp.maximum(jnp.max(jnp.abs(held), axis=1, keepdims=True), 1e-30)
+    coded = jnp.round(held * (CODE_MAX / largest)).astype(jnp.int32).astype(jnp.int16)
+    code_send[...] = coded.reshape(groups, rows, width)
+    stats = jnp.where(lane == 0, top, jnp.where(lane == 1, denom, largest * (1.0 / CODE_MAX)))
+    flipped = stats.T
+    for g in range(groups):
+        stat_send[g, :, 0:rows] = flipped[0:8, g * rows : (g + 1) * rows]
+
+    result_copies = []
+    for number, peer in enumerate(peers):
+        result_copies.append(
+            push(
+                stat_send.at[peer],
+                stat_recv.at[me],
+                stat_send_sem.at[number],
+                stat_recv_sem.at[me],
+                peer,
+            )
+        )
+        result_copies.append(
+            push(
+                code_send.at[peer],
+                code_recv.at[me],
+                code_send_sem.at[number],
+                code_recv_sem.at[me],
+                peer,
+            )
+        )
+    for copy in result_copies:
+        copy.start()
+
+    for number, peer in enumerate(peers):
+        push(
+            cscore_send.at[peer],
+            cscore_recv.at[peer],
+            cscore_send_sem.at[number],
+            cscore_recv_sem.at[peer],
+            peer,
+        ).wait_recv()
+    cscore_recv[me] = cscore_send[me]
+    all_scores = [cscore_recv[g] for g in range(groups)]
+    small_lane = lax.broadcasted_iota(jnp.int32, (rows, LANES), 1)
+    real = small_lane < clusters
+    cmax = functools.reduce(jnp.maximum, [jnp.where(real, s, floor_value) for s in all_scores])
+    cmax = jnp.max(cmax, axis=1, keepdims=True)
+    csum = sum(jnp.where(real, jnp.exp(s - cmax), 0.0) for s in all_scores)
+    lse = cmax + jnp.log(jnp.sum(csum, axis=1, keepdims=True))
+    own_beams = beam_ref[pl.ds(pl.multiple_of(me * rows, rows), rows), :]
+    picks = jnp.zeros((rows, LANES), jnp.float32)
+    for k in range(beam_width):
+        wanted = own_beams[:, k : k + 1]
+        found = sum(
+            jnp.where(real & (wanted == small_lane + g * clusters), s, 0.0)
+            for g, s in enumerate(all_scores)
+        )
+        picks = jnp.where(small_lane == k, jnp.sum(found, axis=1, keepdims=True), picks)
+    logprob_ref[...] = (picks - lse)[:, 0:beam_width]
+
+    for number, peer in enumerate(peers):
+        push(
+            stat_send.at[peer],
+            stat_recv.at[peer],
+            stat_send_sem.at[number],
+            stat_recv_sem.at[peer],
+            peer,
+        ).wait_recv()
+    stat_recv[me] = stat_send[me]
+    code_recv[me] = code_send[me]
+    tops = stat_recv[:, 0, :]
+    overall = jnp.max(tops, axis=0, keepdims=True)
+    factors = jnp.exp(tops - overall)
+    whole = jnp.sum(factors * stat_recv[:, 1, :], axis=0, keepdims=True)
+    shares = factors * stat_recv[:, 2, :] / whole
+    shares = jnp.concatenate(
+        [shares, jnp.zeros((LANES - groups, LANES), jnp.float32)], axis=0
+    ).T[0:rows]
+
+    for number, peer in enumerate(peers):
+        push(
+            code_send.at[peer],
+            code_recv.at[peer],
+            code_send_sem.at[number],
+            code_recv_sem.at[peer],
+            peer,
+        ).wait_recv()
+    merged = jnp.zeros((rows, width), jnp.float32)
+    for g in range(groups):
+        merged = merged + code_recv[g].astype(jnp.int32).astype(jnp.float32) * shares[:, g : g + 1]
+    readout_ref[...] = merged.astype(jnp.bfloat16)
+
+    for copy in sends + cscore_copies + result_copies:
+        copy.wait_send()
+
+
+def fused(queries, centroids, leaves, beam):
+    groups = lax.axis_size("cluster")
+    rows, width = queries.shape
+    clusters = centroids.shape[0]
+    if rows % 16 or groups % 2 or groups > 16 or rows > LANES:
+        return per_device(queries, centroids, leaves, beam)
+    vmem = pl.BlockSpec(memory_space=pltpu.VMEM)
+    dma = pltpu.SemaphoreType.DMA
+    peers = groups - 1
+    return pl.pallas_call(
+        functools.partial(fused_kernel, groups),
+        out_shape=(
+            jax.ShapeDtypeStruct((rows, width), jnp.bfloat16),
+            jax.ShapeDtypeStruct((rows, beam.shape[1]), jnp.float32),
+        ),
+        in_specs=[vmem, vmem, pl.BlockSpec(memory_space=pl.ANY), vmem],
+        out_specs=(vmem, vmem),
+        scratch_shapes=[
+            pltpu.VMEM((groups, rows, width), jnp.bfloat16),
+            pltpu.VMEM(leaves.shape, jnp.bfloat16),
+            pltpu.VMEM((groups, rows, LANES), jnp.float32),
+            pltpu.VMEM((groups, rows, LANES), jnp.float32),
+            pltpu.VMEM((groups, 8, LANES), jnp.float32),
+            pltpu.VMEM((groups, 8, LANES), jnp.float32),
+            pltpu.VMEM((groups, rows, width), jnp.int16),
+            pltpu.VMEM((groups, rows, width), jnp.int16),
+            pltpu.VMEM((groups * rows, width), jnp.float32),
+            dma((clusters,)),
+            dma,
+            dma((groups,)),
+            dma((groups,)),
+            dma((peers,)),
+            dma((groups,)),
+            dma((peers,)),
+            dma((groups,)),
+            dma((peers,)),
+            dma((groups,)),
+        ],
+        compiler_params=pltpu.CompilerParams(
+            collective_id=0, has_side_effects=True, vmem_limit_bytes=48 * 1024 * 1024
+        ),
+    )(queries, centroids, leaves, beam)
+
+
 def solution(mesh):
     return jax.shard_map(
-        per_device,
+        fused,
         mesh=mesh,
         in_specs=(
             P(("query", "cluster"), None),

time: 113 us -> 30.4 us (0.27)
  blocking collectives: 70.6 us -> 0 us
  Pallas kernels: 0 us -> 26 us
  between operations: 14.1 us -> 0.66 us
  other arithmetic: 13.2 us -> 0 us
  matrix products: 12.5 us -> 0 us
  local copies, waits for them, and re-layouts: 1.53 us -> 3.55 us
    all_gather x6 -> x0, blocking collectives: 70.6 us -> none  [the longest x5 54.5 us: merged_2(): gathered = jax.tree.map(lambda a: lax.all_gather(a, axis), part)]
    pallas_call x0 -> x1, Pallas kernels: none -> 26 us  [fused(): pl.pallas_call(functools.partial(fused_kernel, groups), out_shape=(jax.Sh...]
    dot_general x4 -> x0, matrix products: 12.5 us -> none  [the longest x1 5.34 us: per_device(): jnp.einsum('csd,cjd->csj', picked, leaves, preferred_element_type=jnp.flo...]
    add x30 -> x0, other arithmetic: 9.03 us -> none  [the longest x7 8.6 us: combine_states(): accum_one * factor_one[:, None] + accum_two * factor_two[:, None]]
    unnamed x8 -> x6, local copies, waits for them, and re-layouts: 0.02 us -> 2.88 us
    dynamic_slice x21 -> x0, local copies, waits for them, and re-layouts: 1.29 us -> none  [the longest x20 1.21 us: take(): lax.dynamic_index_in_dim(a, source, 0, False)]
    reduce_sum x5 -> x0, other arithmetic: 1.15 us -> none  [the longest x1 0.59 us: per_device(): slot_sum = jnp.sum(weights, axis=2)]
  transfers between devices with their start and end apart: 1 -> 0, of which waited for: 0 -> 0; matrix products, arithmetic and copies ran while one was open for 1% -> 0% of each run, Pallas kernels for 0% -> 0%
where the time goes in v1:
time: 30.4 us; the launch traced here: 30.2 us
  Pallas kernels  26 us (86%)
  local copies, waits for them, and re-layouts  3.55 us (12%)
  between operations  0.66 us (2%)
    pallas_call x1, Pallas kernels, fused(): pl.pallas_call(functools.partial(fused_kernel, groups), out_shape=(jax.Sh...  26 us
    unnamed x6, local copies, waits for them, and re-layouts  2.88 us
    pallas_call x1, local copies, waits for them, and re-layouts, fused(): pl.pallas_call(functools.partial(fused_kernel, groups), out_shape=(jax.Sh...  0.66 us

profile of v1, /device:TPU:0, one launch (start us, length us, event | category | flops | bytes accessed | tf_op | source)
XLA Modules:
  0.0 30.2 jit_solution(8389323203376510246)
XLA Ops:
  0.6 0.8 %copy.6.beam_ref = s32[256,8]{1,0:T(8,128)S(1)} copy(s32[256,8]{0,1:T(8,128)} %param.7) | data formatting | bytes 16384 | tf_op args[3]
  1.5 0.0 copy-start
  1.5 0.8 %copy-done = bf16[32,512]{1,0:T(8,128)(2,1)S(1)} copy-done((bf16[32,512]{1,0:T(8,128)(2,1)S(1)}, bf16[32,512]{1,0:T(8,128)(2,1)}, u32[]{:S(2)}) %copy-start) | copy-done | bytes 32792
  2.2 0.0 copy-start.1
  2.2 0.7 %copy-done.1 = bf16[8,512]{1,0:T(8,128)(2,1)S(1)} copy-done((bf16[8,512]{1,0:T(8,128)(2,1)S(1)}, bf16[8,512]{1,0:T(8,128)(2,1)}, u32[]{:S(2)}) %copy-start.1) | copy-done | bytes 8216
  2.9 26.0 %shard_map.59 = (bf16[32,512]{1,0:T(8,128)(2,1)S(1)}, f32[32,8]{1,0:T(8,128)S(1)}) custom-call(bf16[32,512]{1,0:T(8,128)(2,1)S(1)} %copy-done, bf16[8,512]{1,0:T(8,128)(2,1)S(1)} %copy-done.1, bf16[8,1024,512]{2,1,0:T(8,128)(2,1)} %leaves_ref.1, s32[256,8]{1,0:T(8,128)S(1)} %copy.6.beam_ref), custom_call_target="tpu_custom_call" | custom-call | tf_op jit(solution)/shard_map/pallas_call | solution.py:361
  28.9 0.7 %copy.7 = f32[32,8]{0,1:T(8,128)} copy(f32[32,8]{1,0:T(8,128)S(1)} %get-tuple-element.3) | data formatting | bytes 2048 | tf_op jit(solution)/shard_map/pallas_call | solution.py:361
  29.6 0.6 %copy.9 = bf16[32,512]{1,0:T(8,128)(2,1)} copy(bf16[32,512]{1,0:T(8,128)(2,1)S(1)} %get-tuple-element.6) | data formatting | bytes 65536
Async XLA Ops:
  1.5 0.8 %copy-start = (bf16[32,512]{1,0:T(8,128)(2,1)S(1)}, bf16[32,512]{1,0:T(8,128)(2,1)}, u32[]{:S(2)}) copy-start(bf16[32,512]{1,0:T(8,128)(2,1)} %q_ref.1) | copy-start | bytes 98308
  2.2 0.7 %copy-start.1 = (bf16[8,512]{1,0:T(8,128)(2,1)S(1)}, bf16[8,512]{1,0:T(8,128)(2,1)}, u32[]{:S(2)}) copy-start(bf16[8,512]{1,0:T(8,128)(2,1)} %cent_ref.1) | copy-start | bytes 24580

commit v2 on v1

--- a/solution.py
+++ b/solution.py
@@ -106,6 +106,7 @@
 
 def fused_kernel(
     groups,
+    capacity,
     q_ref,
     cent_ref,
     leaves_ref,
@@ -113,20 +114,21 @@
     readout_ref,
     logprob_ref,
     block,
+    cent_buf,
+    beam_buf,
     leaf_buf,
-    cscore_send,
-    cscore_recv,
+    centroid_send,
+    centroid_recv,
     stat_send,
     stat_recv,
     code_send,
     code_recv,
-    accum,
     leaf_sem,
     own_sem,
     q_send_sem,
     q_recv_sem,
-    cscore_send_sem,
-    cscore_recv_sem,
+    centroid_send_sem,
+    centroid_recv_sem,
     stat_send_sem,
     stat_recv_sem,
     code_send_sem,
@@ -135,9 +137,10 @@
     rows, width = q_ref.shape
     clusters = cent_ref.shape[0]
     total = groups * rows
-    beam_width = beam_ref.shape[1]
+    beam_width = beam_ref.shape[0]
     chips = groups // 2
     score_scale = 1.0 / math.sqrt(width)
+    f32 = jnp.float32
     me = lax.axis_index("cluster")
     chip, core = me // 2, me % 2
     sibling = chip * 2 + (1 - core)
@@ -148,19 +151,24 @@
 
     peers = [peer_at(o, s) for o in range(1, chips) for s in (core, 1 - core)] + [sibling]
 
+    def signal_peers():
+        barrier = pltpu.get_barrier_semaphore()
+        for peer in peers:
+            pl.semaphore_signal(barrier, inc=1, device_id={"cluster": peer}, device_id_type=MESH)
+        pl.semaphore_wait(barrier, len(peers))
+
+    own_copies = [
+        pltpu.make_async_copy(q_ref, block.at[me], own_sem.at[0]),
+        pltpu.make_async_copy(beam_ref, beam_buf, own_sem.at[1]),
+        pltpu.make_async_copy(cent_ref, cent_buf, own_sem.at[2]),
+    ]
     leaf_copies = [
         pltpu.make_async_copy(leaves_ref.at[c], leaf_buf.at[c], leaf_sem.at[c])
         for c in range(clusters)
     ]
-    for copy in leaf_copies:
+    for copy in own_copies + leaf_copies:
         copy.start()
-    own_copy = pltpu.make_async_copy(q_ref, block.at[me], own_sem)
-    own_copy.start()
-
-    barrier = pltpu.get_barrier_semaphore()
-    for peer in peers:
-        pl.semaphore_signal(barrier, inc=1, device_id={"cluster": peer}, device_id_type=MESH)
-    pl.semaphore_wait(barrier, len(peers))
+    signal_peers()
 
     def push(src, dst, send_sem, recv_sem, peer):
         return pltpu.make_async_remote_copy(
@@ -172,13 +180,44 @@
             device_id_type=MESH,
         )
 
+    own_copies[0].wait()
+    mine = block.at[me]
     sends = []
     for number, offset in enumerate(range(1, chips)):
         peer = peer_at(offset, core)
-        sends.append(push(q_ref, block.at[me], q_send_sem.at[number], q_recv_sem.at[me], peer))
-    sends.append(push(q_ref, block.at[me], q_send_sem.at[chips - 1], q_recv_sem.at[me], sibling))
+        sends.append(push(mine, mine, q_send_sem.at[number], q_recv_sem.at[me], peer))
+    sends.append(push(mine, mine, q_send_sem.at[chips - 1], q_recv_sem.at[me], sibling))
     for copy in sends:
         copy.start()
+
+    own_copies[1].wait()
+    beams = beam_buf[...]
+    members = jnp.concatenate(
+        [
+            jnp.max((beams == first + c).astype(f32), axis=0, keepdims=True)
+            for c in range(clusters)
+        ],
+        axis=0,
+    )
+    upper = (
+        lax.broadcasted_iota(jnp.int32, (total, total), 0)
+        <= lax.broadcasted_iota(jnp.int32, (total, total), 1)
+    ).astype(jnp.bfloat16)
+    padded = jnp.concatenate([members, jnp.zeros((LANES - clusters, total), f32)], axis=0)
+    counts = jnp.dot(padded.astype(jnp.bfloat16), upper, preferred_element_type=f32)
+    slots = jnp.where(padded > 0.0, counts, 0.0)
+    slot_number = lax.broadcasted_iota(jnp.int32, (capacity, total), 0).astype(f32) + 1.0
+    dispatch = jnp.concatenate(
+        [(slots[c : c + 1, :] == slot_number).astype(f32) for c in range(clusters)], axis=0
+    )
+    slot_total = clusters * capacity
+    slots_down = slots.T
+    slot_across = lax.broadcasted_iota(jnp.int32, (total, slot_total), 1)
+    wanted = jnp.concatenate(
+        [jnp.broadcast_to(slots_down[:, c : c + 1], (total, capacity)) for c in range(clusters)],
+        axis=1,
+    )
+    collect = (wanted == (slot_across % capacity).astype(f32) + 1.0).astype(jnp.bfloat16)
 
     def arrival(origin):
         return push(block.at[origin], block.at[origin], q_send_sem.at[0], q_recv_sem.at[origin], sibling)
@@ -198,70 +237,93 @@
     arrival(sibling).wait_recv()
     for offset in range(1, chips):
         arrival(peer_at(chips - offset, 1 - core)).wait_recv()
-    own_copy.wait()
+    own_copies[2].wait()
 
     queries = block[...].reshape(total, width)
-    lane = lax.broadcasted_iota(jnp.int32, (total, LANES), 1)
     cent = jnp.concatenate(
-        [cent_ref[...], jnp.zeros((LANES - clusters, width), cent_ref.dtype)], axis=0
+        [cent_buf[...], jnp.zeros((LANES - clusters, width), cent_buf.dtype)], axis=0
     )
     nt = (((1,), (1,)), ((), ()))
-    cscore = lax.dot_general(queries, cent, nt, preferred_element_type=jnp.float32) * score_scale
-    cscore_send[...] = cscore.reshape(groups, rows, LANES)
-
-    cscore_copies = []
-    for number, peer in enumerate(peers):
-        cscore_copies.append(
-            push(
-                cscore_send.at[peer],
-                cscore_recv.at[me],
-                cscore_send_sem.at[number],
-                cscore_recv_sem.at[me],
-                peer,
-            )
-        )
-    for copy in cscore_copies:
+    cscore = lax.dot_general(cent, queries, nt, preferred_element_type=f32)[0:clusters]
+    cscore = cscore * score_scale
+    part_max = jnp.max(cscore, axis=0, keepdims=True)
+    part_sum = jnp.sum(jnp.exp(cscore - part_max), axis=0, keepdims=True)
+    picks = sum(
+        jnp.where(beams == first + c, cscore[c : c + 1, :], 0.0) for c in range(clusters)
+    )
+    for g in range(groups):
+        lanes = slice(g * rows, (g + 1) * rows)
+        centroid_send[g, 0:beam_width, 0:rows] = picks[:, lanes]
+        centroid_send[g, beam_width : beam_width + 1, 0:rows] = part_max[:, lanes]
+        centroid_send[g, beam_width + 1 : beam_width + 2, 0:rows] = part_sum[:, lanes]
+    centroid_copies = [
+        push(
+            centroid_send.at[peer],
+            centroid_recv.at[me],
+            centroid_send_sem.at[number],
+            centroid_recv_sem.at[me],
+            peer,
+        )
+        for number, peer in enumerate(peers)
+    ]
+    for copy in centroid_copies:
         copy.start()
 
-    beams = beam_ref[...]
-    top = jnp.full((total, 1), floor_value, jnp.float32)
-    denom = jnp.zeros((total, 1), jnp.float32)
+    picked = jnp.dot(
+        dispatch.astype(jnp.bfloat16), queries, preferred_element_type=f32
+    ).astype(jnp.bfloat16)
+    lane = lax.broadcasted_iota(jnp.int32, (slot_total, LANES), 1)
+    owner = lax.broadcasted_iota(jnp.int32, (slot_total, LANES), 0) // capacity
+    slot_scores = lax.dot_general(picked, cent, nt, preferred_element_type=f32) * score_scale
+    slot_centroid = jnp.sum(jnp.where(lane == owner, slot_scores, 0.0), axis=1, keepdims=True)
+    for copy in leaf_copies:
+        copy.wait()
 
     def scores(c):
-        leaf_copies[c].wait()
-        return lax.dot_general(queries, leaf_buf[c], nt, preferred_element_type=jnp.float32)
-
+        return lax.dot_general(
+            picked[c * capacity : (c + 1) * capacity],
+            leaf_buf[c],
+            nt,
+            preferred_element_type=f32,
+        )
+
+    peaks, masses, sums = [], [], []
     current = scores(0)
     for c in range(clusters):
         upcoming = scores(c + 1) if c + 1 < clusters else None
-        member = jnp.max((beams == first + c).astype(jnp.float32), axis=1, keepdims=True) > 0.0
-        centroid = jnp.sum(jnp.where(lane == c, cscore, 0.0), axis=1, keepdims=True)
         peak = jnp.max(current, axis=1, keepdims=True)
         weights = jnp.exp((current - peak) * score_scale)
-        mass = jnp.sum(weights, axis=1, keepdims=True)
-        summed = jnp.dot(
-            weights.astype(jnp.bfloat16), leaf_buf[c], preferred_element_type=jnp.float32
-        )
-        level = jnp.where(member, peak * score_scale + centroid, floor_value)
-        raised = jnp.maximum(top, level)
-        keep = jnp.exp(top - raised)
-        gain = jnp.where(member, jnp.exp(level - raised), 0.0)
-        denom = denom * keep + mass * gain
-        if c == 0:
-            accum[...] = summed * gain
-        else:
-            accum[...] = accum[...] * keep + summed * gain
-        top = raised
+        masses.append(jnp.sum(weights, axis=1, keepdims=True))
+        peaks.append(peak)
+        sums.append(
+            jnp.dot(weights.astype(jnp.bfloat16), leaf_buf[c], preferred_element_type=f32)
+        )
         current = upcoming
-
-    held = accum[...]
+    level = jnp.concatenate(peaks, axis=0) * score_scale + slot_centroid
+    mass = jnp.concatenate(masses, axis=0)
+    summed = jnp.concatenate(sums, axis=0)
+
+    used = dispatch > 0.0
+    top = jnp.max(jnp.where(used, level, floor_value), axis=0, keepdims=True)
+    slot_top = jnp.max(jnp.where(used, top, floor_value), axis=1, keepdims=True)
+    filled = jnp.max(dispatch, axis=1, keepdims=True) > 0.0
+    gain = jnp.where(filled, jnp.exp(jnp.where(filled, level - slot_top, 0.0)), 0.0)
+    denom = jnp.sum(jnp.where(used, mass * gain, 0.0), axis=0, keepdims=True)
+    scaled = summed * gain
+    coarse = scaled.astype(jnp.bfloat16)
+    fine = (scaled - coarse.astype(f32)).astype(jnp.bfloat16)
+    held = jnp.dot(collect, coarse, preferred_element_type=f32) + jnp.dot(
+        collect, fine, preferred_element_type=f32
+    )
     largest = jnp.maximum(jnp.max(jnp.abs(held), axis=1, keepdims=True), 1e-30)
     coded = jnp.round(held * (CODE_MAX / largest)).astype(jnp.int32).astype(jnp.int16)
     code_send[...] = coded.reshape(groups, rows, width)
-    stats = jnp.where(lane == 0, top, jnp.where(lane == 1, denom, largest * (1.0 / CODE_MAX)))
-    flipped = stats.T
+    steps = jnp.broadcast_to(largest * (1.0 / CODE_MAX), (total, LANES)).T
     for g in range(groups):
-        stat_send[g, :, 0:rows] = flipped[0:8, g * rows : (g + 1) * rows]
+        lanes = slice(g * rows, (g + 1) * rows)
+        stat_send[g, 0:1, 0:rows] = top[:, lanes]
+        stat_send[g, 1:2, 0:rows] = denom[:, lanes]
+        stat_send[g, 2:3, 0:rows] = steps[0:1, lanes]
 
     result_copies = []
     for number, peer in enumerate(peers):
@@ -288,30 +350,21 @@
 
     for number, peer in enumerate(peers):
         push(
-            cscore_send.at[peer],
-            cscore_recv.at[peer],
-            cscore_send_sem.at[number],
-            cscore_recv_sem.at[peer],
+            centroid_send.at[peer],
+            centroid_recv.at[peer],
+            centroid_send_sem.at[number],
+            centroid_recv_sem.at[peer],
             peer,
         ).wait_recv()
-    cscore_recv[me] = cscore_send[me]
-    all_scores = [cscore_recv[g] for g in range(groups)]
-    small_lane = lax.broadcasted_iota(jnp.int32, (rows, LANES), 1)
-    real = small_lane < clusters
-    cmax = functools.reduce(jnp.maximum, [jnp.where(real, s, floor_value) for s in all_scores])
-    cmax = jnp.max(cmax, axis=1, keepdims=True)
-    csum = sum(jnp.where(real, jnp.exp(s - cmax), 0.0) for s in all_scores)
-    lse = cmax + jnp.log(jnp.sum(csum, axis=1, keepdims=True))
-    own_beams = beam_ref[pl.ds(pl.multiple_of(me * rows, rows), rows), :]
-    picks = jnp.zeros((rows, LANES), jnp.float32)
-    for k in range(beam_width):
-        wanted = own_beams[:, k : k + 1]
-        found = sum(
-            jnp.where(real & (wanted == small_lane + g * clusters), s, 0.0)
-            for g, s in enumerate(all_scores)
-        )
-        picks = jnp.where(small_lane == k, jnp.sum(found, axis=1, keepdims=True), picks)
-    logprob_ref[...] = (picks - lse)[:, 0:beam_width]
+    centroid_recv[me] = centroid_send[me]
+    parts = [centroid_recv[g] for g in range(groups)]
+    cmax = functools.reduce(jnp.maximum, [p[beam_width : beam_width + 1] for p in parts])
+    csum = sum(
+        p[beam_width + 1 : beam_width + 2] * jnp.exp(p[beam_width : beam_width + 1] - cmax)
+        for p in parts
+    )
+    logprob = sum(p[0:beam_width] for p in parts) - (cmax + jnp.log(csum))
+    logprob_ref[...] = logprob[:, 0:rows]
 
     for number, peer in enumerate(peers):
         push(
@@ -328,9 +381,7 @@
     factors = jnp.exp(tops - overall)
     whole = jnp.sum(factors * stat_recv[:, 1, :], axis=0, keepdims=True)
     shares = factors * stat_recv[:, 2, :] / whole
-    shares = jnp.concatenate(
-        [shares, jnp.zeros((LANES - groups, LANES), jnp.float32)], axis=0
-    ).T[0:rows]
+    shares = jnp.concatenate([shares, jnp.zeros((LANES - groups, LANES), f32)], axis=0).T[0:rows]
 
     for number, peer in enumerate(peers):
         push(
@@ -340,12 +391,12 @@
             code_recv_sem.at[peer],
             peer,
         ).wait_recv()
-    merged = jnp.zeros((rows, width), jnp.float32)
+    merged = jnp.zeros((rows, width), f32)
     for g in range(groups):
-        merged = merged + code_recv[g].astype(jnp.int32).astype(jnp.float32) * shares[:, g : g + 1]
+        merged = merged + code_recv[g].astype(jnp.int32).astype(f32) * shares[:, g : g + 1]
     readout_ref[...] = merged.astype(jnp.bfloat16)
 
-    for copy in sends + cscore_copies + result_copies:
+    for copy in sends + centroid_copies + result_copies:
         copy.wait_send()
 
 
@@ -353,31 +404,35 @@
     groups = lax.axis_size("cluster")
     rows, width = queries.shape
     clusters = centroids.shape[0]
-    if rows % 16 or groups % 2 or groups > 16 or rows > LANES:
+    total, beam_width = beam.shape
+    capacity = 2 * total * beam_width // (clusters * groups)
+    if rows % 16 or capacity % 16 or groups % 2 or groups > 16 or rows > LANES or beam_width != 8:
         return per_device(queries, centroids, leaves, beam)
     vmem = pl.BlockSpec(memory_space=pltpu.VMEM)
+    hbm = pl.BlockSpec(memory_space=pltpu.HBM)
     dma = pltpu.SemaphoreType.DMA
     peers = groups - 1
-    return pl.pallas_call(
-        functools.partial(fused_kernel, groups),
+    readout, logprob = pl.pallas_call(
+        functools.partial(fused_kernel, groups, capacity),
         out_shape=(
             jax.ShapeDtypeStruct((rows, width), jnp.bfloat16),
-            jax.ShapeDtypeStruct((rows, beam.shape[1]), jnp.float32),
+            jax.ShapeDtypeStruct((beam_width, rows), jnp.float32),
         ),
-        in_specs=[vmem, vmem, pl.BlockSpec(memory_space=pl.ANY), vmem],
+        in_specs=[hbm, hbm, hbm, hbm],
         out_specs=(vmem, vmem),
         scratch_shapes=[
             pltpu.VMEM((groups, rows, width), jnp.bfloat16),
+            pltpu.VMEM(centroids.shape, jnp.bfloat16),
+            pltpu.VMEM((beam_width, total), jnp.int32),
             pltpu.VMEM(leaves.shape, jnp.bfloat16),
-            pltpu.VMEM((groups, rows, LANES), jnp.float32),
-            pltpu.VMEM((groups, rows, LANES), jnp.float32),
+            pltpu.VMEM((groups, beam_width + 8, LANES), jnp.float32),
+            pltpu.VMEM((groups, beam_width + 8, LANES), jnp.float32),
             pltpu.VMEM((groups, 8, LANES), jnp.float32),
             pltpu.VMEM((groups, 8, LANES), jnp.float32),
             pltpu.VMEM((groups, rows, width), jnp.int16),
             pltpu.VMEM((groups, rows, width), jnp.int16),
-            pltpu.VMEM((groups * rows, width), jnp.float32),
             dma((clusters,)),
-            dma,
+            dma((3,)),
             dma((groups,)),
             dma((groups,)),
             dma((peers,)),
@@ -388,9 +443,10 @@
             dma((groups,)),
         ],
         compiler_params=pltpu.CompilerParams(
-            collective_id=0, has_side_effects=True, vmem_limit_bytes=48 * 1024 * 1024
+            collective_id=0, has_side_effects=True, vmem_limit_bytes=64 * 1024 * 1024
         ),
-    )(queries, centroids, leaves, beam)
+    )(queries, centroids, leaves, beam.T)
+    return readout, logprob.T
 
 
 def solution(mesh):

time: 30.4 us -> 28.1 us (0.924)
  Pallas kernels: 26 us -> 24.6 us
  local copies, waits for them, and re-layouts: 3.55 us -> 2.65 us
    pallas_call x1, Pallas kernels: 26 us -> 24.6 us  [fused(): pl.pallas_call(functools.partial(fused_kernel, groups, capacity), out_sha...]
    pallas_call x1 -> x0, local copies, waits for them, and re-layouts: 0.66 us -> none  [fused(): pl.pallas_call(functools.partial(fused_kernel, groups), out_shape=(jax.Sh...]
    unnamed x6 -> x2, local copies, waits for them, and re-layouts: 2.88 us -> 2.65 us
where the time goes in v2:
time: 28.1 us; the launch traced here: 27.9 us
  Pallas kernels  24.6 us (88%)
  local copies, waits for them, and re-layouts  2.65 us (9%)
  between operations  0.64 us (2%)
    pallas_call x1, Pallas kernels, fused(): pl.pallas_call(functools.partial(fused_kernel, groups, capacity), out_sha...  24.6 us
    unnamed x2, local copies, waits for them, and re-layouts  2.65 us

profile of v2, /device:TPU:0, one launch (start us, length us, event | category | flops | bytes accessed | tf_op | source)
XLA Modules:
  0.0 27.9 jit_solution(7464339924903139435)
XLA Ops:
  0.6 24.6 %shard_map.59 = (bf16[32,512]{1,0:T(8,128)(2,1)}, f32[8,32]{1,0:T(8,128)}) custom-call(bf16[32,512]{1,0:T(8,128)(2,1)} %q_ref.1, bf16[8,512]{1,0:T(8,128)(2,1)} %cent_ref.1, bf16[8,1024,512]{2,1,0:T(8,128)(2,1)} %leaves_ref.1, s32[8,256]{1,0:T(8,128)} %bitcast.2), custom_call_target="tpu_custom_call" | custom-call | tf_op jit(solution)/shard_map/pallas_call | solution.py:415
  25.3 1.4 %copy.8 = bf16[32,512]{1,0:T(8,128)(2,1)} copy(bf16[32,512]{1,0:T(8,128)(2,1)} %get-tuple-element.8) | data formatting | bytes 65536
  26.6 1.3 %copy.9 = f32[32,8]{0,1:T(8,128)} copy(f32[32,8]{0,1:T(8,128)} %bitcast.3) | data formatting | bytes 2048

commit v3 on v2

--- a/solution.py
+++ b/solution.py
@@ -119,6 +119,10 @@
     leaf_buf,
     centroid_send,
     centroid_recv,
+    held_buf,
+    near_recv,
+    level_buf,
+    near_level,
     stat_send,
     stat_recv,
     code_send,
@@ -129,6 +133,8 @@
     q_recv_sem,
     centroid_send_sem,
     centroid_recv_sem,
+    near_send_sem,
+    near_recv_sem,
     stat_send_sem,
     stat_recv_sem,
     code_send_sem,
@@ -315,38 +321,81 @@
     held = jnp.dot(collect, coarse, preferred_element_type=f32) + jnp.dot(
         collect, fine, preferred_element_type=f32
     )
-    largest = jnp.maximum(jnp.max(jnp.abs(held), axis=1, keepdims=True), 1e-30)
-    coded = jnp.round(held * (CODE_MAX / largest)).astype(jnp.int32).astype(jnp.int16)
-    code_send[...] = coded.reshape(groups, rows, width)
-    steps = jnp.broadcast_to(largest * (1.0 / CODE_MAX), (total, LANES)).T
     for g in range(groups):
         lanes = slice(g * rows, (g + 1) * rows)
-        stat_send[g, 0:1, 0:rows] = top[:, lanes]
-        stat_send[g, 1:2, 0:rows] = denom[:, lanes]
-        stat_send[g, 2:3, 0:rows] = steps[0:1, lanes]
+        level_buf[g % 2, g // 2, 0:1, 0:rows] = top[:, lanes]
+        level_buf[g % 2, g // 2, 1:2, 0:rows] = denom[:, lanes]
+        held_buf[g % 2, g // 2] = held[lanes]
+    order = [2, 1, 3, 0] if chips == 4 else list(range(1, chips)) + [0]
+    near_copies = [
+        push(
+            level_buf.at[1 - core],
+            near_level,
+            near_send_sem.at[chips],
+            near_recv_sem.at[chips],
+            sibling,
+        )
+    ]
+    for offset in order:
+        g = lax.rem(chip + offset, chips)
+        near_copies.append(
+            push(
+                held_buf.at[1 - core, g],
+                near_recv.at[g],
+                near_send_sem.at[offset],
+                near_recv_sem.at[g],
+                sibling,
+            )
+        )
+    for copy in near_copies:
+        copy.start()
+
+    near_copies[0].wait_recv()
+    diagonal = lax.broadcasted_iota(jnp.int32, (rows, LANES), 0) == lax.broadcasted_iota(
+        jnp.int32, (rows, LANES), 1
+    )
+
+    def to_column(row):
+        return jnp.sum(jnp.where(diagonal, row, 0.0), axis=1, keepdims=True)
+
+    def to_row(column):
+        return jnp.sum(jnp.where(diagonal, column, 0.0), axis=0, keepdims=True)
 
     result_copies = []
-    for number, peer in enumerate(peers):
-        result_copies.append(
-            push(
-                stat_send.at[peer],
-                stat_recv.at[me],
-                stat_send_sem.at[number],
-                stat_recv_sem.at[me],
-                peer,
+    for number, offset in enumerate(order):
+        g = lax.rem(chip + offset, chips)
+        here, near = level_buf[core, g], near_level[g]
+        high = jnp.maximum(here[0:1], near[0:1])
+        here_gain, near_gain = jnp.exp(here[0:1] - high), jnp.exp(near[0:1] - high)
+        amount = here[1:2] * here_gain + near[1:2] * near_gain
+        push(
+            held_buf.at[1 - core, g],
+            near_recv.at[g],
+            near_send_sem.at[offset],
+            near_recv_sem.at[g],
+            sibling,
+        ).wait_recv()
+        both = held_buf[core, g] * to_column(here_gain) + near_recv[g] * to_column(near_gain)
+        if offset == 0:
+            own_high, own_amount, own_both = high, amount, both
+            continue
+        largest = jnp.maximum(jnp.max(jnp.abs(both), axis=1, keepdims=True), 1e-30)
+        code_send[number] = (
+            jnp.round(both * (CODE_MAX / largest)).astype(jnp.int32).astype(jnp.int16)
+        )
+        stat_send[number, 0:1] = high
+        stat_send[number, 1:2] = amount
+        stat_send[number, 2:3] = to_row(largest * (1.0 / CODE_MAX))
+        peer = g * 2 + core
+        for buffers, sems in (
+            ((stat_send, stat_recv), (stat_send_sem, stat_recv_sem)),
+            ((code_send, code_recv), (code_send_sem, code_recv_sem)),
+        ):
+            copy = push(
+                buffers[0].at[number], buffers[1].at[chip], sems[0].at[number], sems[1].at[chip], peer
             )
-        )
-        result_copies.append(
-            push(
-                code_send.at[peer],
-                code_recv.at[me],
-                code_send_sem.at[number],
-                code_recv_sem.at[me],
-                peer,
-            )
-        )
-    for copy in result_copies:
-        copy.start()
+            copy.start()
+            result_copies.append(copy)
 
     for number, peer in enumerate(peers):
         push(
@@ -366,38 +415,35 @@
     logprob = sum(p[0:beam_width] for p in parts) - (cmax + jnp.log(csum))
     logprob_ref[...] = logprob[:, 0:rows]
 
-    for number, peer in enumerate(peers):
-        push(
-            stat_send.at[peer],
-            stat_recv.at[peer],
-            stat_send_sem.at[number],
-            stat_recv_sem.at[peer],
-            peer,
-        ).wait_recv()
-    stat_recv[me] = stat_send[me]
-    code_recv[me] = code_send[me]
-    tops = stat_recv[:, 0, :]
-    overall = jnp.max(tops, axis=0, keepdims=True)
-    factors = jnp.exp(tops - overall)
-    whole = jnp.sum(factors * stat_recv[:, 1, :], axis=0, keepdims=True)
-    shares = factors * stat_recv[:, 2, :] / whole
-    shares = jnp.concatenate([shares, jnp.zeros((LANES - groups, LANES), f32)], axis=0).T[0:rows]
-
-    for number, peer in enumerate(peers):
-        push(
-            code_send.at[peer],
-            code_recv.at[peer],
-            code_send_sem.at[number],
-            code_recv_sem.at[peer],
-            peer,
-        ).wait_recv()
-    merged = jnp.zeros((rows, width), f32)
-    for g in range(groups):
-        merged = merged + code_recv[g].astype(jnp.int32).astype(f32) * shares[:, g : g + 1]
+    sources = [lax.rem(chip + offset, chips) for offset in range(1, chips)]
+    for g in sources:
+        push(stat_send.at[0], stat_recv.at[g], stat_send_sem.at[0], stat_recv_sem.at[g], sibling).wait_recv()
+    stats = [stat_recv[g] for g in sources]
+    overall = functools.reduce(jnp.maximum, [t[0:1] for t in stats], own_high)
+    own_share = jnp.exp(own_high - overall)
+    shares = [jnp.exp(t[0:1] - overall) for t in stats]
+    whole = own_amount * own_share + sum(f * t[1:2] for f, t in zip(shares, stats))
+    merged = own_both * to_column(own_share / whole)
+    for g, share, stat in zip(sources, shares, stats):
+        push(code_send.at[0], code_recv.at[g], code_send_sem.at[0], code_recv_sem.at[g], sibling).wait_recv()
+        merged = merged + code_recv[g].astype(jnp.int32).astype(f32) * to_column(
+            share * stat[2:3] / whole
+        )
     readout_ref[...] = merged.astype(jnp.bfloat16)
 
-    for copy in sends + centroid_copies + result_copies:
+    for copy in sends + centroid_copies + near_copies + result_copies:
         copy.wait_send()
+
+
+def store_kernel(readout_ref, logprob_ref, readout_out, logprob_out, sems):
+    copies = [
+        pltpu.make_async_copy(readout_ref, readout_out, sems.at[0]),
+        pltpu.make_async_copy(logprob_ref, logprob_out, sems.at[1]),
+    ]
+    for copy in copies:
+        copy.start()
+    for copy in copies:
+        copy.wait()
 
 
 def fused(queries, centroids, leaves, beam):
@@ -412,6 +458,7 @@
     hbm = pl.BlockSpec(memory_space=pltpu.HBM)
     dma = pltpu.SemaphoreType.DMA
     peers = groups - 1
+    chips = groups // 2
     readout, logprob = pl.pallas_call(
         functools.partial(fused_kernel, groups, capacity),
         out_shape=(
@@ -427,25 +474,42 @@
             pltpu.VMEM(leaves.shape, jnp.bfloat16),
             pltpu.VMEM((groups, beam_width + 8, LANES), jnp.float32),
             pltpu.VMEM((groups, beam_width + 8, LANES), jnp.float32),
-            pltpu.VMEM((groups, 8, LANES), jnp.float32),
-            pltpu.VMEM((groups, 8, LANES), jnp.float32),
-            pltpu.VMEM((groups, rows, width), jnp.int16),
-            pltpu.VMEM((groups, rows, width), jnp.int16),
+            pltpu.VMEM((2, chips, rows, width), jnp.float32),
+            pltpu.VMEM((chips, rows, width), jnp.float32),
+            pltpu.VMEM((2, chips, 8, LANES), jnp.float32),
+            pltpu.VMEM((chips, 8, LANES), jnp.float32),
+            pltpu.VMEM((chips, 8, LANES), jnp.float32),
+            pltpu.VMEM((chips, 8, LANES), jnp.float32),
+            pltpu.VMEM((chips, rows, width), jnp.int16),
+            pltpu.VMEM((chips, rows, width), jnp.int16),
             dma((clusters,)),
             dma((3,)),
             dma((groups,)),
             dma((groups,)),
             dma((peers,)),
             dma((groups,)),
-            dma((peers,)),
-            dma((groups,)),
-            dma((peers,)),
-            dma((groups,)),
+            dma((chips + 1,)),
+            dma((chips + 1,)),
+            dma((chips,)),
+            dma((chips,)),
+            dma((chips,)),
+            dma((chips,)),
         ],
         compiler_params=pltpu.CompilerParams(
             collective_id=0, has_side_effects=True, vmem_limit_bytes=64 * 1024 * 1024
         ),
     )(queries, centroids, leaves, beam.T)
+    readout, logprob = pl.pallas_call(
+        store_kernel,
+        out_shape=(
+            jax.ShapeDtypeStruct(readout.shape, readout.dtype),
+            jax.ShapeDtypeStruct(logprob.shape, logprob.dtype),
+        ),
+        in_specs=[hbm, hbm],
+        out_specs=(hbm, hbm),
+        scratch_shapes=[dma((2,))],
+        compiler_params=pltpu.CompilerParams(vmem_limit_bytes=64 * 1024 * 1024),
+    )(readout, logprob)
     return readout, logprob.T
 
 

time: 28.1 us -> 26.4 us (0.940)
  local copies, waits for them, and re-layouts: 2.65 us -> 0 us
  Pallas kernels: 24.6 us -> 25.6 us
    unnamed x2 -> x0, local copies, waits for them, and re-layouts: 2.65 us -> none
    pallas_call x0 -> x1, Pallas kernels: none -> 2.24 us  [fused(): pl.pallas_call(store_kernel, out_shape=(jax.ShapeDtypeStruct(readout.shap...]
    pallas_call x1, Pallas kernels: 24.6 us -> 23.4 us  [fused(): pl.pallas_call(functools.partial(fused_kernel, groups, capacity), out_sha...]
where the time goes in v3:
time: 26.4 us; the launch traced here: 26.3 us
  Pallas kernels  25.6 us (97%)
  between operations  0.64 us (2%)
    pallas_call x1, Pallas kernels, fused(): pl.pallas_call(functools.partial(fused_kernel, groups, capacity), out_sha...  23.4 us
    pallas_call x1, Pallas kernels, fused(): pl.pallas_call(store_kernel, out_shape=(jax.ShapeDtypeStruct(readout.shap...  2.24 us

profile of v3, /device:TPU:0, one launch (start us, length us, event | category | flops | bytes accessed | tf_op | source)
XLA Modules:
  0.0 26.3 jit_solution(10086913293562108700)
XLA Ops:
  0.6 23.4 %shard_map.59 = (bf16[32,512]{1,0:T(8,128)(2,1)}, f32[8,32]{1,0:T(8,128)}) custom-call(bf16[32,512]{1,0:T(8,128)(2,1)} %q_ref.1, bf16[8,512]{1,0:T(8,128)(2,1)} %cent_ref.1, bf16[8,1024,512]{2,1,0:T(8,128)(2,1)} %leaves_ref.1, s32[8,256]{1,0:T(8,128)} %bitcast.2), custom_call_target="tpu_custom_call" | custom-call | tf_op jit(solution)/shard_map/pallas_call | solution.py:462
  24.0 2.2 %shard_map.60 = (bf16[32,512]{1,0:T(8,128)(2,1)}, f32[8,32]{1,0:T(8,128)}) custom-call(bf16[32,512]{1,0:T(8,128)(2,1)} %get-tuple-element.6.readout_ref, f32[8,32]{1,0:T(8,128)} %get-tuple-element.7.logprob_ref), custom_call_target="tpu_custom_call" | custom-call | tf_op jit(solution)/shard_map/pallas_call | solution.py:502

commit v4 on v3

--- a/solution.py
+++ b/solution.py
@@ -117,6 +117,8 @@
     cent_buf,
     beam_buf,
     leaf_buf,
+    partial_buf,
+    weight_buf,
     centroid_send,
     centroid_recv,
     held_buf,
@@ -145,6 +147,7 @@
     total = groups * rows
     beam_width = beam_ref.shape[0]
     chips = groups // 2
+    half = width // 2
     score_scale = 1.0 / math.sqrt(width)
     f32 = jnp.float32
     me = lax.axis_index("cluster")
@@ -164,9 +167,11 @@
         pl.semaphore_wait(barrier, len(peers))
 
     own_copies = [
-        pltpu.make_async_copy(q_ref, block.at[me], own_sem.at[0]),
-        pltpu.make_async_copy(beam_ref, beam_buf, own_sem.at[1]),
-        pltpu.make_async_copy(cent_ref, cent_buf, own_sem.at[2]),
+        pltpu.make_async_copy(q_ref.at[:, h * half : (h + 1) * half], block.at[h, me], own_sem.at[h])
+        for h in range(2)
+    ] + [
+        pltpu.make_async_copy(beam_ref, beam_buf, own_sem.at[2]),
+        pltpu.make_async_copy(cent_ref, cent_buf, own_sem.at[3]),
     ]
     leaf_copies = [
         pltpu.make_async_copy(leaves_ref.at[c], leaf_buf.at[c], leaf_sem.at[c])
@@ -186,17 +191,20 @@
             device_id_type=MESH,
         )
 
-    own_copies[0].wait()
-    mine = block.at[me]
     sends = []
-    for number, offset in enumerate(range(1, chips)):
-        peer = peer_at(offset, core)
-        sends.append(push(mine, mine, q_send_sem.at[number], q_recv_sem.at[me], peer))
-    sends.append(push(mine, mine, q_send_sem.at[chips - 1], q_recv_sem.at[me], sibling))
-    for copy in sends:
-        copy.start()
-
-    own_copies[1].wait()
+    for h in range(2):
+        own_copies[h].wait()
+        mine = block.at[h, me]
+        for number, offset in enumerate(range(1, chips)):
+            peer = peer_at(offset, core)
+            sends.append(push(mine, mine, q_send_sem.at[h, number], q_recv_sem.at[h, me], peer))
+            sends[-1].start()
+        sends.append(
+            push(mine, mine, q_send_sem.at[h, chips - 1], q_recv_sem.at[h, me], sibling)
+        )
+        sends[-1].start()
+
+    own_copies[2].wait()
     beams = beam_buf[...]
     members = jnp.concatenate(
         [
@@ -225,32 +233,66 @@
     )
     collect = (wanted == (slot_across % capacity).astype(f32) + 1.0).astype(jnp.bfloat16)
 
-    def arrival(origin):
-        return push(block.at[origin], block.at[origin], q_send_sem.at[0], q_recv_sem.at[origin], sibling)
-
-    for offset in range(1, chips):
-        origin = peer_at(chips - offset, core)
-        arrival(origin).wait_recv()
-        relay = push(
-            block.at[origin],
-            block.at[origin],
-            q_send_sem.at[chips - 1 + offset],
-            q_recv_sem.at[origin],
-            sibling,
+    def arrival(h, origin):
+        place = block.at[h, origin]
+        return push(place, place, q_send_sem.at[h, 0], q_recv_sem.at[h, origin], sibling)
+
+    def relay_half(h):
+        for offset in range(1, chips):
+            origin = peer_at(chips - offset, core)
+            arrival(h, origin).wait_recv()
+            place = block.at[h, origin]
+            relay = push(
+                place,
+                place,
+                q_send_sem.at[h, chips - 1 + offset],
+                q_recv_sem.at[h, origin],
+                sibling,
+            )
+            relay.start()
+            sends.append(relay)
+
+    def finish_half(h):
+        arrival(h, sibling).wait_recv()
+        for offset in range(1, chips):
+            arrival(h, peer_at(chips - offset, 1 - core)).wait_recv()
+        return block[h].reshape(total, half)
+
+    nt = (((1,), (1,)), ((), ()))
+    dispatch_low = dispatch.astype(jnp.bfloat16)
+
+    def pick(rows_of):
+        return jnp.dot(dispatch_low, rows_of, preferred_element_type=f32).astype(jnp.bfloat16)
+
+    def scores(picked, c, h):
+        return lax.dot_general(
+            picked[c * capacity : (c + 1) * capacity],
+            leaf_buf[c, :, h * half : (h + 1) * half],
+            nt,
+            preferred_element_type=f32,
         )
-        relay.start()
-        sends.append(relay)
-    arrival(sibling).wait_recv()
-    for offset in range(1, chips):
-        arrival(peer_at(chips - offset, 1 - core)).wait_recv()
-    own_copies[2].wait()
-
-    queries = block[...].reshape(total, width)
+
+    relay_half(0)
+    queries_low = finish_half(0)
+    picked_low = pick(queries_low)
+    for c in range(clusters // 2):
+        leaf_copies[c].wait()
+    for c in range(clusters // 2):
+        partial_buf[c] = scores(picked_low, c, 0)
+    relay_half(1)
+    for c in range(clusters // 2, clusters):
+        leaf_copies[c].wait()
+    for c in range(clusters // 2, clusters):
+        partial_buf[c] = scores(picked_low, c, 0)
+    own_copies[3].wait()
+    queries_high = finish_half(1)
     cent = jnp.concatenate(
         [cent_buf[...], jnp.zeros((LANES - clusters, width), cent_buf.dtype)], axis=0
     )
-    nt = (((1,), (1,)), ((), ()))
-    cscore = lax.dot_general(cent, queries, nt, preferred_element_type=f32)[0:clusters]
+    cscore = (
+        lax.dot_general(cent[:, 0:half], queries_low, nt, preferred_element_type=f32)
+        + lax.dot_general(cent[:, half:], queries_high, nt, preferred_element_type=f32)
+    )[0:clusters]
     cscore = cscore * score_scale
     part_max = jnp.max(cscore, axis=0, keepdims=True)
     part_sum = jnp.sum(jnp.exp(cscore - part_max), axis=0, keepdims=True)
@@ -275,39 +317,37 @@
     for copy in centroid_copies:
         copy.start()
 
-    picked = jnp.dot(
-        dispatch.astype(jnp.bfloat16), queries, preferred_element_type=f32
-    ).astype(jnp.bfloat16)
+    picked_high = pick(queries_high)
     lane = lax.broadcasted_iota(jnp.int32, (slot_total, LANES), 1)
     owner = lax.broadcasted_iota(jnp.int32, (slot_total, LANES), 0) // capacity
-    slot_scores = lax.dot_general(picked, cent, nt, preferred_element_type=f32) * score_scale
+    slot_scores = (
+        lax.dot_general(picked_low, cent[:, 0:half], nt, preferred_element_type=f32)
+        + lax.dot_general(picked_high, cent[:, half:], nt, preferred_element_type=f32)
+    ) * score_scale
     slot_centroid = jnp.sum(jnp.where(lane == owner, slot_scores, 0.0), axis=1, keepdims=True)
-    for copy in leaf_copies:
-        copy.wait()
-
-    def scores(c):
-        return lax.dot_general(
-            picked[c * capacity : (c + 1) * capacity],
-            leaf_buf[c],
-            nt,
+
+    def weigh(c, h):
+        return jnp.dot(
+            weight_buf[c],
+            leaf_buf[c, :, h * half : (h + 1) * half],
             preferred_element_type=f32,
         )
 
     peaks, masses, sums = [], [], []
-    current = scores(0)
+    current = partial_buf[0] + scores(picked_high, 0, 1)
     for c in range(clusters):
-        upcoming = scores(c + 1) if c + 1 < clusters else None
+        upcoming = None
+        if c + 1 < clusters:
+            upcoming = partial_buf[c + 1] + scores(picked_high, c + 1, 1)
         peak = jnp.max(current, axis=1, keepdims=True)
         weights = jnp.exp((current - peak) * score_scale)
         masses.append(jnp.sum(weights, axis=1, keepdims=True))
         peaks.append(peak)
-        sums.append(
-            jnp.dot(weights.astype(jnp.bfloat16), leaf_buf[c], preferred_element_type=f32)
-        )
+        weight_buf[c] = weights.astype(jnp.bfloat16)
+        sums.append(weigh(c, 0))
         current = upcoming
     level = jnp.concatenate(peaks, axis=0) * score_scale + slot_centroid
     mass = jnp.concatenate(masses, axis=0)
-    summed = jnp.concatenate(sums, axis=0)
 
     used = dispatch > 0.0
     top = jnp.max(jnp.where(used, level, floor_value), axis=0, keepdims=True)
@@ -315,42 +355,44 @@
     filled = jnp.max(dispatch, axis=1, keepdims=True) > 0.0
     gain = jnp.where(filled, jnp.exp(jnp.where(filled, level - slot_top, 0.0)), 0.0)
     denom = jnp.sum(jnp.where(used, mass * gain, 0.0), axis=0, keepdims=True)
-    scaled = summed * gain
-    coarse = scaled.astype(jnp.bfloat16)
-    fine = (scaled - coarse.astype(f32)).astype(jnp.bfloat16)
-    held = jnp.dot(collect, coarse, preferred_element_type=f32) + jnp.dot(
-        collect, fine, preferred_element_type=f32
-    )
     for g in range(groups):
         lanes = slice(g * rows, (g + 1) * rows)
         level_buf[g % 2, g // 2, 0:1, 0:rows] = top[:, lanes]
         level_buf[g % 2, g // 2, 1:2, 0:rows] = denom[:, lanes]
-        held_buf[g % 2, g // 2] = held[lanes]
     order = [2, 1, 3, 0] if chips == 4 else list(range(1, chips)) + [0]
-    near_copies = [
-        push(
-            level_buf.at[1 - core],
-            near_level,
-            near_send_sem.at[chips],
-            near_recv_sem.at[chips],
+    level_copy = push(
+        level_buf.at[1 - core],
+        near_level,
+        near_send_sem.at[0, chips],
+        near_recv_sem.at[0, chips],
+        sibling,
+    )
+    level_copy.start()
+    near_copies = [level_copy]
+
+    def near_copy(h, offset):
+        g = lax.rem(chip + offset, chips)
+        return push(
+            held_buf.at[h, 1 - core, g],
+            near_recv.at[h, g],
+            near_send_sem.at[h, offset],
+            near_recv_sem.at[h, g],
             sibling,
         )
-    ]
-    for offset in order:
-        g = lax.rem(chip + offset, chips)
-        near_copies.append(
-            push(
-                held_buf.at[1 - core, g],
-                near_recv.at[g],
-                near_send_sem.at[offset],
-                near_recv_sem.at[g],
-                sibling,
-            )
+
+    def share_half(h, sums):
+        scaled = jnp.concatenate(sums, axis=0) * gain
+        coarse = scaled.astype(jnp.bfloat16)
+        fine = (scaled - coarse.astype(f32)).astype(jnp.bfloat16)
+        held = jnp.dot(collect, coarse, preferred_element_type=f32) + jnp.dot(
+            collect, fine, preferred_element_type=f32
         )
-    for copy in near_copies:
-        copy.start()
-
-    near_copies[0].wait_recv()
+        for g in range(groups):
+            held_buf[h, g % 2, g // 2] = held[g * rows : (g + 1) * rows]
+        for offset in order:
+            near_copies.append(near_copy(h, offset))
+            near_copies[-1].start()
+
     diagonal = lax.broadcasted_iota(jnp.int32, (rows, LANES), 0) == lax.broadcasted_iota(
         jnp.int32, (rows, LANES), 1
     )
@@ -362,40 +404,57 @@
         return jnp.sum(jnp.where(diagonal, column, 0.0), axis=0, keepdims=True)
 
     result_copies = []
-    for number, offset in enumerate(order):
-        g = lax.rem(chip + offset, chips)
-        here, near = level_buf[core, g], near_level[g]
-        high = jnp.maximum(here[0:1], near[0:1])
-        here_gain, near_gain = jnp.exp(here[0:1] - high), jnp.exp(near[0:1] - high)
-        amount = here[1:2] * here_gain + near[1:2] * near_gain
-        push(
-            held_buf.at[1 - core, g],
-            near_recv.at[g],
-            near_send_sem.at[offset],
-            near_recv_sem.at[g],
-            sibling,
-        ).wait_recv()
-        both = held_buf[core, g] * to_column(here_gain) + near_recv[g] * to_column(near_gain)
-        if offset == 0:
-            own_high, own_amount, own_both = high, amount, both
-            continue
-        largest = jnp.maximum(jnp.max(jnp.abs(both), axis=1, keepdims=True), 1e-30)
-        code_send[number] = (
-            jnp.round(both * (CODE_MAX / largest)).astype(jnp.int32).astype(jnp.int16)
-        )
-        stat_send[number, 0:1] = high
-        stat_send[number, 1:2] = amount
-        stat_send[number, 2:3] = to_row(largest * (1.0 / CODE_MAX))
-        peer = g * 2 + core
-        for buffers, sems in (
-            ((stat_send, stat_recv), (stat_send_sem, stat_recv_sem)),
-            ((code_send, code_recv), (code_send_sem, code_recv_sem)),
-        ):
-            copy = push(
-                buffers[0].at[number], buffers[1].at[chip], sems[0].at[number], sems[1].at[chip], peer
+
+    def chip_levels():
+        level_copy.wait_recv()
+        found = []
+        for offset in order:
+            g = lax.rem(chip + offset, chips)
+            here, near = level_buf[core, g], near_level[g]
+            high = jnp.maximum(here[0:1], near[0:1])
+            here_gain, near_gain = jnp.exp(here[0:1] - high), jnp.exp(near[0:1] - high)
+            amount = here[1:2] * here_gain + near[1:2] * near_gain
+            found.append((high, amount, to_column(here_gain), to_column(near_gain)))
+        return found
+
+    def merge_half(h, levels):
+        for number, offset in enumerate(order):
+            g = lax.rem(chip + offset, chips)
+            high, amount, here_gain, near_gain = levels[number]
+            near_copy(h, offset).wait_recv()
+            both = held_buf[h, core, g] * here_gain + near_recv[h, g] * near_gain
+            if offset == 0:
+                return both
+            largest = jnp.maximum(jnp.max(jnp.abs(both), axis=1, keepdims=True), 1e-30)
+            code_send[h, number] = (
+                jnp.round(both * (CODE_MAX / largest)).astype(jnp.int32).astype(jnp.int16)
             )
-            copy.start()
-            result_copies.append(copy)
+            stat_send[h, number, 0:1] = high
+            stat_send[h, number, 1:2] = amount
+            stat_send[h, number, 2:3] = to_row(largest * (1.0 / CODE_MAX))
+            peer = g * 2 + core
+            for source, target, send_sem, recv_sem in (
+                (stat_send, stat_recv, stat_send_sem, stat_recv_sem),
+                (code_send, code_recv, code_send_sem, code_recv_sem),
+            ):
+                copy = push(
+                    source.at[h, number],
+                    target.at[h, chip],
+                    send_sem.at[h, number],
+                    recv_sem.at[h, chip],
+                    peer,
+                )
+                copy.start()
+                result_copies.append(copy)
+
+    share_half(0, sums)
+    sums_high = [weigh(c, 1) for c in range(clusters // 2)]
+    levels = chip_levels()
+    own_low = merge_half(0, levels)
+    sums_high += [weigh(c, 1) for c in range(clusters // 2, clusters)]
+    share_half(1, sums_high)
+    own_high_half = merge_half(1, levels)
+    own_top, own_amount = levels[-1][0], levels[-1][1]
 
     for number, peer in enumerate(peers):
         push(
@@ -416,20 +475,35 @@
     logprob_ref[...] = logprob[:, 0:rows]
 
     sources = [lax.rem(chip + offset, chips) for offset in range(1, chips)]
-    for g in sources:
-        push(stat_send.at[0], stat_recv.at[g], stat_send_sem.at[0], stat_recv_sem.at[g], sibling).wait_recv()
-    stats = [stat_recv[g] for g in sources]
-    overall = functools.reduce(jnp.maximum, [t[0:1] for t in stats], own_high)
-    own_share = jnp.exp(own_high - overall)
-    shares = [jnp.exp(t[0:1] - overall) for t in stats]
-    whole = own_amount * own_share + sum(f * t[1:2] for f, t in zip(shares, stats))
-    merged = own_both * to_column(own_share / whole)
-    for g, share, stat in zip(sources, shares, stats):
-        push(code_send.at[0], code_recv.at[g], code_send_sem.at[0], code_recv_sem.at[g], sibling).wait_recv()
-        merged = merged + code_recv[g].astype(jnp.int32).astype(f32) * to_column(
-            share * stat[2:3] / whole
-        )
-    readout_ref[...] = merged.astype(jnp.bfloat16)
+    own_share = whole = None
+    for h, own in enumerate((own_low, own_high_half)):
+        for g in sources:
+            push(
+                stat_send.at[h, 0],
+                stat_recv.at[h, g],
+                stat_send_sem.at[h, 0],
+                stat_recv_sem.at[h, g],
+                sibling,
+            ).wait_recv()
+        stats = [stat_recv[h, g] for g in sources]
+        if h == 0:
+            overall = functools.reduce(jnp.maximum, [t[0:1] for t in stats], own_top)
+            own_share = jnp.exp(own_top - overall)
+            shares = [jnp.exp(t[0:1] - overall) for t in stats]
+            whole = own_amount * own_share + sum(f * t[1:2] for f, t in zip(shares, stats))
+        merged = own * to_column(own_share / whole)
+        for g, share, stat in zip(sources, shares, stats):
+            push(
+                code_send.at[h, 0],
+                code_recv.at[h, g],
+                code_send_sem.at[h, 0],
+                code_recv_sem.at[h, g],
+                sibling,
+            ).wait_recv()
+            merged = merged + code_recv[h, g].astype(jnp.int32).astype(f32) * to_column(
+                share * stat[2:3] / whole
+            )
+        readout_ref[:, h * half : (h + 1) * half] = merged.astype(jnp.bfloat16)
 
     for copy in sends + centroid_copies + near_copies + result_copies:
         copy.wait_send()
@@ -452,13 +526,14 @@
     clusters = centroids.shape[0]
     total, beam_width = beam.shape
     capacity = 2 * total * beam_width // (clusters * groups)
-    if rows % 16 or capacity % 16 or groups % 2 or groups > 16 or rows > LANES or beam_width != 8:
+    if rows % 16 or capacity % 16 or groups % 2 or groups > 16 or rows > LANES or beam_width != 8 or width % 256:
         return per_device(queries, centroids, leaves, beam)
     vmem = pl.BlockSpec(memory_space=pltpu.VMEM)
     hbm = pl.BlockSpec(memory_space=pltpu.HBM)
     dma = pltpu.SemaphoreType.DMA
     peers = groups - 1
     chips = groups // 2
+    half = width // 2
     readout, logprob = pl.pallas_call(
         functools.partial(fused_kernel, groups, capacity),
         out_shape=(
@@ -468,32 +543,34 @@
         in_specs=[hbm, hbm, hbm, hbm],
         out_specs=(vmem, vmem),
         scratch_shapes=[
-            pltpu.VMEM((groups, rows, width), jnp.bfloat16),
+            pltpu.VMEM((2, groups, rows, half), jnp.bfloat16),
             pltpu.VMEM(centroids.shape, jnp.bfloat16),
             pltpu.VMEM((beam_width, total), jnp.int32),
             pltpu.VMEM(leaves.shape, jnp.bfloat16),
+            pltpu.VMEM((clusters, capacity, leaves.shape[1]), jnp.float32),
+            pltpu.VMEM((clusters, capacity, leaves.shape[1]), jnp.bfloat16),
             pltpu.VMEM((groups, beam_width + 8, LANES), jnp.float32),
             pltpu.VMEM((groups, beam_width + 8, LANES), jnp.float32),
-            pltpu.VMEM((2, chips, rows, width), jnp.float32),
-            pltpu.VMEM((chips, rows, width), jnp.float32),
+            pltpu.VMEM((2, 2, chips, rows, half), jnp.float32),
+            pltpu.VMEM((2, chips, rows, half), jnp.float32),
             pltpu.VMEM((2, chips, 8, LANES), jnp.float32),
             pltpu.VMEM((chips, 8, LANES), jnp.float32),
-            pltpu.VMEM((chips, 8, LANES), jnp.float32),
-            pltpu.VMEM((chips, 8, LANES), jnp.float32),
-            pltpu.VMEM((chips, rows, width), jnp.int16),
-            pltpu.VMEM((chips, rows, width), jnp.int16),
+            pltpu.VMEM((2, chips, 8, LANES), jnp.float32),
+            pltpu.VMEM((2, chips, 8, LANES), jnp.float32),
+            pltpu.VMEM((2, chips, rows, half), jnp.int16),
+            pltpu.VMEM((2, chips, rows, half), jnp.int16),
             dma((clusters,)),
-            dma((3,)),
-            dma((groups,)),
-            dma((groups,)),
+            dma((4,)),
+            dma((2, groups)),
+            dma((2, groups)),
             dma((peers,)),
             dma((groups,)),
-            dma((chips + 1,)),
-            dma((chips + 1,)),
-            dma((chips,)),
-            dma((chips,)),
-            dma((chips,)),
-            dma((chips,)),
+            dma((2, chips + 1)),
+            dma((2, chips + 1)),
+            dma((2, chips)),
+            dma((2, chips)),
+            dma((2, chips)),
+            dma((2, chips)),
         ],
         compiler_params=pltpu.CompilerParams(
             collective_id=0, has_side_effects=True, vmem_limit_bytes=64 * 1024 * 1024

time: 26.4 us -> 27.6 us (1.045)
  Pallas kernels: 25.6 us -> 26.8 us
    pallas_call x1, Pallas kernels: 23.4 us -> 24.5 us  [fused(): pl.pallas_call(functools.partial(fused_kernel, groups, capacity), out_sha...]
where the time goes in v4:
time: 27.6 us; the launch traced here: 27.4 us
  Pallas kernels  26.8 us (97%)
  between operations  0.64 us (2%)
    pallas_call x1, Pallas kernels, fused(): pl.pallas_call(functools.partial(fused_kernel, groups, capacity), out_sha...  24.5 us
    pallas_call x1, Pallas kernels, fused(): pl.pallas_call(store_kernel, out_shape=(jax.ShapeDtypeStruct(readout.shap...  2.24 us

profile of v4, /device:TPU:0, one launch (start us, length us, event | category | flops | bytes accessed | tf_op | source)
XLA Modules:
  0.0 27.4 jit_solution(17592964323343197469)
XLA Ops:
  0.6 24.5 %shard_map.59 = (bf16[32,512]{1,0:T(8,128)(2,1)}, f32[8,32]{1,0:T(8,128)}) custom-call(bf16[32,512]{1,0:T(8,128)(2,1)} %q_ref.1, bf16[8,512]{1,0:T(8,128)(2,1)} %cent_ref.1, bf16[8,1024,512]{2,1,0:T(8,128)(2,1)} %leaves_ref.1, s32[8,256]{1,0:T(8,128)} %bitcast.2), custom_call_target="tpu_custom_call" | custom-call | tf_op jit(solution)/shard_map/pallas_call | solution.py:537
  25.2 2.2 %shard_map.60 = (bf16[32,512]{1,0:T(8,128)(2,1)}, f32[8,32]{1,0:T(8,128)}) custom-call(bf16[32,512]{1,0:T(8,128)(2,1)} %get-tuple-element.6.readout_ref, f32[8,32]{1,0:T(8,128)} %get-tuple-element.7.logprob_ref), custom_call_target="tpu_custom_call" | custom-call | tf_op jit(solution)/shard_map/pallas_call | solution.py:579

commit v5 on v3

--- a/solution.py
+++ b/solution.py
@@ -287,22 +287,34 @@
 
     def scores(c):
         return lax.dot_general(
+            leaf_buf[c],
             picked[c * capacity : (c + 1) * capacity],
-            leaf_buf[c],
             nt,
             preferred_element_type=f32,
         )
+
+    slot_diagonal = lax.broadcasted_iota(
+        jnp.int32, (capacity, capacity), 0
+    ) == lax.broadcasted_iota(jnp.int32, (capacity, capacity), 1)
+
+    def slot_column(row):
+        return jnp.sum(jnp.where(slot_diagonal, row, 0.0), axis=1, keepdims=True)
 
     peaks, masses, sums = [], [], []
     current = scores(0)
     for c in range(clusters):
         upcoming = scores(c + 1) if c + 1 < clusters else None
-        peak = jnp.max(current, axis=1, keepdims=True)
+        peak = jnp.max(current, axis=0, keepdims=True)
         weights = jnp.exp((current - peak) * score_scale)
-        masses.append(jnp.sum(weights, axis=1, keepdims=True))
-        peaks.append(peak)
+        masses.append(slot_column(jnp.sum(weights, axis=0, keepdims=True)))
+        peaks.append(slot_column(peak))
         sums.append(
-            jnp.dot(weights.astype(jnp.bfloat16), leaf_buf[c], preferred_element_type=f32)
+            lax.dot_general(
+                weights.astype(jnp.bfloat16),
+                leaf_buf[c],
+                (((0,), (0,)), ((), ())),
+                preferred_element_type=f32,
+            )
         )
         current = upcoming
     level = jnp.concatenate(peaks, axis=0) * score_scale + slot_centroid

time: 26.4 us -> 27.2 us (1.030)
  Pallas kernels: 25.6 us -> 26.4 us
    pallas_call x1, Pallas kernels: 23.4 us -> 24.2 us  [fused(): pl.pallas_call(functools.partial(fused_kernel, groups, capacity), out_sha...]
where the time goes in v5:
time: 27.2 us; the launch traced here: 27.1 us
  Pallas kernels  26.4 us (97%)
  between operations  0.64 us (2%)
    pallas_call x1, Pallas kernels, fused(): pl.pallas_call(functools.partial(fused_kernel, groups, capacity), out_sha...  24.2 us
    pallas_call x1, Pallas kernels, fused(): pl.pallas_call(store_kernel, out_shape=(jax.ShapeDtypeStruct(readout.shap...  2.24 us

profile of v5, /device:TPU:0, one launch (start us, length us, event | category | flops | bytes accessed | tf_op | source)
XLA Modules:
  0.0 27.1 jit_solution(6010918532462903200)
XLA Ops:
  0.6 24.2 %shard_map.59 = (bf16[32,512]{1,0:T(8,128)(2,1)}, f32[8,32]{1,0:T(8,128)}) custom-call(bf16[32,512]{1,0:T(8,128)(2,1)} %q_ref.1, bf16[8,512]{1,0:T(8,128)(2,1)} %cent_ref.1, bf16[8,1024,512]{2,1,0:T(8,128)(2,1)} %leaves_ref.1, s32[8,256]{1,0:T(8,128)} %bitcast.2), custom_call_target="tpu_custom_call" | custom-call | tf_op jit(solution)/shard_map/pallas_call | solution.py:474
  24.8 2.2 %shard_map.60 = (bf16[32,512]{1,0:T(8,128)(2,1)}, f32[8,32]{1,0:T(8,128)}) custom-call(bf16[32,512]{1,0:T(8,128)(2,1)} %get-tuple-element.6.readout_ref, f32[8,32]{1,0:T(8,128)} %get-tuple-element.7.logprob_ref), custom_call_target="tpu_custom_call" | custom-call | tf_op jit(solution)/shard_map/pallas_call | solution.py:514

commit v6 on v4

--- a/solution.py
+++ b/solution.py
@@ -117,7 +117,6 @@
     cent_buf,
     beam_buf,
     leaf_buf,
-    partial_buf,
     weight_buf,
     centroid_send,
     centroid_recv,
@@ -167,11 +166,9 @@
         pl.semaphore_wait(barrier, len(peers))
 
     own_copies = [
-        pltpu.make_async_copy(q_ref.at[:, h * half : (h + 1) * half], block.at[h, me], own_sem.at[h])
-        for h in range(2)
-    ] + [
-        pltpu.make_async_copy(beam_ref, beam_buf, own_sem.at[2]),
-        pltpu.make_async_copy(cent_ref, cent_buf, own_sem.at[3]),
+        pltpu.make_async_copy(q_ref, block.at[me], own_sem.at[0]),
+        pltpu.make_async_copy(beam_ref, beam_buf, own_sem.at[1]),
+        pltpu.make_async_copy(cent_ref, cent_buf, own_sem.at[2]),
     ]
     leaf_copies = [
         pltpu.make_async_copy(leaves_ref.at[c], leaf_buf.at[c], leaf_sem.at[c])
@@ -191,20 +188,17 @@
             device_id_type=MESH,
         )
 
+    own_copies[0].wait()
+    mine = block.at[me]
     sends = []
-    for h in range(2):
-        own_copies[h].wait()
-        mine = block.at[h, me]
-        for number, offset in enumerate(range(1, chips)):
-            peer = peer_at(offset, core)
-            sends.append(push(mine, mine, q_send_sem.at[h, number], q_recv_sem.at[h, me], peer))
-            sends[-1].start()
-        sends.append(
-            push(mine, mine, q_send_sem.at[h, chips - 1], q_recv_sem.at[h, me], sibling)
-        )
-        sends[-1].start()
-
-    own_copies[2].wait()
+    for number, offset in enumerate(range(1, chips)):
+        peer = peer_at(offset, core)
+        sends.append(push(mine, mine, q_send_sem.at[number], q_recv_sem.at[me], peer))
+    sends.append(push(mine, mine, q_send_sem.at[chips - 1], q_recv_sem.at[me], sibling))
+    for copy in sends:
+        copy.start()
+
+    own_copies[1].wait()
     beams = beam_buf[...]
     members = jnp.concatenate(
         [
@@ -233,66 +227,32 @@
     )
     collect = (wanted == (slot_across % capacity).astype(f32) + 1.0).astype(jnp.bfloat16)
 
-    def arrival(h, origin):
-        place = block.at[h, origin]
-        return push(place, place, q_send_sem.at[h, 0], q_recv_sem.at[h, origin], sibling)
-
-    def relay_half(h):
-        for offset in range(1, chips):
-            origin = peer_at(chips - offset, core)
-            arrival(h, origin).wait_recv()
-            place = block.at[h, origin]
-            relay = push(
-                place,
-                place,
-                q_send_sem.at[h, chips - 1 + offset],
-                q_recv_sem.at[h, origin],
-                sibling,
-            )
-            relay.start()
-            sends.append(relay)
-
-    def finish_half(h):
-        arrival(h, sibling).wait_recv()
-        for offset in range(1, chips):
-            arrival(h, peer_at(chips - offset, 1 - core)).wait_recv()
-        return block[h].reshape(total, half)
-
-    nt = (((1,), (1,)), ((), ()))
-    dispatch_low = dispatch.astype(jnp.bfloat16)
-
-    def pick(rows_of):
-        return jnp.dot(dispatch_low, rows_of, preferred_element_type=f32).astype(jnp.bfloat16)
-
-    def scores(picked, c, h):
-        return lax.dot_general(
-            picked[c * capacity : (c + 1) * capacity],
-            leaf_buf[c, :, h * half : (h + 1) * half],
-            nt,
-            preferred_element_type=f32,
-        )
-
-    relay_half(0)
-    queries_low = finish_half(0)
-    picked_low = pick(queries_low)
-    for c in range(clusters // 2):
-        leaf_copies[c].wait()
-    for c in range(clusters // 2):
-        partial_buf[c] = scores(picked_low, c, 0)
-    relay_half(1)
-    for c in range(clusters // 2, clusters):
-        leaf_copies[c].wait()
-    for c in range(clusters // 2, clusters):
-        partial_buf[c] = scores(picked_low, c, 0)
-    own_copies[3].wait()
-    queries_high = finish_half(1)
+    def arrival(origin):
+        return push(block.at[origin], block.at[origin], q_send_sem.at[0], q_recv_sem.at[origin], sibling)
+
+    for offset in range(1, chips):
+        origin = peer_at(chips - offset, core)
+        arrival(origin).wait_recv()
+        relay = push(
+            block.at[origin],
+            block.at[origin],
+            q_send_sem.at[chips - 1 + offset],
+            q_recv_sem.at[origin],
+            sibling,
+        )
+        relay.start()
+        sends.append(relay)
+    arrival(sibling).wait_recv()
+    for offset in range(1, chips):
+        arrival(peer_at(chips - offset, 1 - core)).wait_recv()
+    own_copies[2].wait()
+
+    queries = block[...].reshape(total, width)
     cent = jnp.concatenate(
         [cent_buf[...], jnp.zeros((LANES - clusters, width), cent_buf.dtype)], axis=0
     )
-    cscore = (
-        lax.dot_general(cent[:, 0:half], queries_low, nt, preferred_element_type=f32)
-        + lax.dot_general(cent[:, half:], queries_high, nt, preferred_element_type=f32)
-    )[0:clusters]
+    nt = (((1,), (1,)), ((), ()))
+    cscore = lax.dot_general(cent, queries, nt, preferred_element_type=f32)[0:clusters]
     cscore = cscore * score_scale
     part_max = jnp.max(cscore, axis=0, keepdims=True)
     part_sum = jnp.sum(jnp.exp(cscore - part_max), axis=0, keepdims=True)
@@ -317,14 +277,23 @@
     for copy in centroid_copies:
         copy.start()
 
-    picked_high = pick(queries_high)
+    picked = jnp.dot(
+        dispatch.astype(jnp.bfloat16), queries, preferred_element_type=f32
+    ).astype(jnp.bfloat16)
     lane = lax.broadcasted_iota(jnp.int32, (slot_total, LANES), 1)
     owner = lax.broadcasted_iota(jnp.int32, (slot_total, LANES), 0) // capacity
-    slot_scores = (
-        lax.dot_general(picked_low, cent[:, 0:half], nt, preferred_element_type=f32)
-        + lax.dot_general(picked_high, cent[:, half:], nt, preferred_element_type=f32)
-    ) * score_scale
+    slot_scores = lax.dot_general(picked, cent, nt, preferred_element_type=f32) * score_scale
     slot_centroid = jnp.sum(jnp.where(lane == owner, slot_scores, 0.0), axis=1, keepdims=True)
+    for copy in leaf_copies:
+        copy.wait()
+
+    def scores(c):
+        return lax.dot_general(
+            picked[c * capacity : (c + 1) * capacity],
+            leaf_buf[c],
+            nt,
+            preferred_element_type=f32,
+        )
 
     def weigh(c, h):
         return jnp.dot(
@@ -334,11 +303,9 @@
         )
 
     peaks, masses, sums = [], [], []
-    current = partial_buf[0] + scores(picked_high, 0, 1)
+    current = scores(0)
     for c in range(clusters):
-        upcoming = None
-        if c + 1 < clusters:
-            upcoming = partial_buf[c + 1] + scores(picked_high, c + 1, 1)
+        upcoming = scores(c + 1) if c + 1 < clusters else None
         peak = jnp.max(current, axis=1, keepdims=True)
         weights = jnp.exp((current - peak) * score_scale)
         masses.append(jnp.sum(weights, axis=1, keepdims=True))
@@ -543,11 +510,10 @@
         in_specs=[hbm, hbm, hbm, hbm],
         out_specs=(vmem, vmem),
         scratch_shapes=[
-            pltpu.VMEM((2, groups, rows, half), jnp.bfloat16),
+            pltpu.VMEM((groups, rows, width), jnp.bfloat16),
             pltpu.VMEM(centroids.shape, jnp.bfloat16),
             pltpu.VMEM((beam_width, total), jnp.int32),
             pltpu.VMEM(leaves.shape, jnp.bfloat16),
-            pltpu.VMEM((clusters, capacity, leaves.shape[1]), jnp.float32),
             pltpu.VMEM((clusters, capacity, leaves.shape[1]), jnp.bfloat16),
             pltpu.VMEM((groups, beam_width + 8, LANES), jnp.float32),
             pltpu.VMEM((groups, beam_width + 8, LANES), jnp.float32),
@@ -560,9 +526,9 @@
             pltpu.VMEM((2, chips, rows, half), jnp.int16),
             pltpu.VMEM((2, chips, rows, half), jnp.int16),
             dma((clusters,)),
-            dma((4,)),
-            dma((2, groups)),
-            dma((2, groups)),
+            dma((3,)),
+            dma((groups,)),
+            dma((groups,)),
             dma((peers,)),
             dma((groups,)),
             dma((2, chips + 1)),

time: 27.6 us -> 27.7 us (level)
  no operation moved by 1% of the time
where the time goes in v6:
time: 27.7 us; the launch traced here: 27.5 us
  Pallas kernels  26.9 us (97%)
  between operations  0.64 us (2%)
    pallas_call x1, Pallas kernels, fused(): pl.pallas_call(functools.partial(fused_kernel, groups, capacity), out_sha...  24.7 us
    pallas_call x1, Pallas kernels, fused(): pl.pallas_call(store_kernel, out_shape=(jax.ShapeDtypeStruct(readout.shap...  2.24 us

profile of v6, /device:TPU:0, one launch (start us, length us, event | category | flops | bytes accessed | tf_op | source)
XLA Modules:
  0.0 27.5 jit_solution(10127447929680462304)
XLA Ops:
  0.6 24.7 %shard_map.59 = (bf16[32,512]{1,0:T(8,128)(2,1)}, f32[8,32]{1,0:T(8,128)}) custom-call(bf16[32,512]{1,0:T(8,128)(2,1)} %q_ref.1, bf16[8,512]{1,0:T(8,128)(2,1)} %cent_ref.1, bf16[8,1024,512]{2,1,0:T(8,128)(2,1)} %leaves_ref.1, s32[8,256]{1,0:T(8,128)} %bitcast.2), custom_call_target="tpu_custom_call" | custom-call | tf_op jit(solution)/shard_map/pallas_call | solution.py:504
  25.3 2.2 %shard_map.60 = (bf16[32,512]{1,0:T(8,128)(2,1)}, f32[8,32]{1,0:T(8,128)}) custom-call(bf16[32,512]{1,0:T(8,128)(2,1)} %get-tuple-element.6.readout_ref, f32[8,32]{1,0:T(8,128)} %get-tuple-element.7.logprob_ref), custom_call_target="tpu_custom_call" | custom-call | tf_op jit(solution)/shard_map/pallas_call | solution.py:545
